TPU v7x, 512 devices: a whole 4x8x8 slice. The times are simulated.
512 devices in a mesh: dap: 64 (over y, z_lo, core), ch: 8 (over x, z_hi).
Axes of the slice: x: 4, y: 8, z: 8 (z_hi: 2, z_lo: 4; z = z_hi * 4 + z_lo), core: 2. Of those that a mesh axis runs over, the one named last changes fastest.
Arguments:
- pair: bfloat16 [128, 512, 512], P('ch', 'dap'), may hold values from -25 to 25
- pair_mask: int32 [512, 512], P('dap'), may hold values 0 or 1
- in_gain: float32 [128], replicated, may hold values from 0.1 to 1.9
- in_bias: float32 [128], replicated, may hold values from -3 to 3
- ab_weight: bfloat16 [4, 128, 128], P(None, None, 'ch'), may hold values from -2 to 2
- hid_gain: float32 [128], P('ch'), may hold values from 0.1 to 1.9
- hid_bias: float32 [128], P('ch'), may hold values from -3 to 3
- out_weight: bfloat16 [128, 128], P('ch'), may hold values from -0.5 to 0.5
- gate_weight: bfloat16 [128, 128], P(None, 'ch'), may hold values from -0.5 to 0.5
Outputs:
- update_t: bfloat16 [128, 512, 512], P('ch', 'dap')
All inputs are finite; a program needn't handle non-finite values. No bound on the sum of `pair_mask` on one device may be relied on, other than what follows from the above.
Results may differ from a plain program's by a relative error of at most 0.0055.
Values may be sent and summed in bfloat16 or wider, within the bound.
A program may use at most 64 MiB of HBM per device.

v0:
```python
import jax
import jax.numpy as jnp
from jax import lax
from jax.sharding import PartitionSpec as P

PAIR_CH = 128
TRI_CH = 128


EPS = 1e-05


def normalize(values, total, squares, count, gain, bias):
    mean = total / count
    var = squares / count - mean * mean
    return (values - mean) * lax.rsqrt(var + EPS) * gain[:, None, None] + bias[:, None, None]


def body(pair, pair_mask, in_gain, in_bias, ab_weight, hid_gain, hid_bias, out_weight, gate_weight):
    own_ch = pair.shape[0]
    rows = pair.shape[1]
    width = pair.shape[2]
    offset = lax.axis_index("ch") * own_ch
    floats = pair.astype(jnp.float32)
    total, squares = lax.psum((jnp.sum(floats, 0), jnp.sum(floats * floats, 0)), "ch")
    gain = lax.dynamic_slice_in_dim(in_gain, offset, own_ch, 0)
    bias = lax.dynamic_slice_in_dim(in_bias, offset, own_ch, 0)
    own_norm = normalize(floats, total, squares, PAIR_CH, gain, bias).astype(jnp.bfloat16)
    z_ln = lax.all_gather(own_norm, "ch", axis=0, tiled=True)
    flat = z_ln.reshape(PAIR_CH, rows * width)
    proj = jnp.einsum("mch,cx->mhx", ab_weight, flat, preferred_element_type=jnp.float32)
    masking = pair_mask.astype(jnp.float32).reshape(-1)
    hidden_ch = proj.shape[1]
    left = (
        (jax.nn.sigmoid(proj[0]) * proj[1] * masking)
        .astype(jnp.bfloat16)
        .reshape(hidden_ch, rows, width)
    )
    right = (
        (jax.nn.sigmoid(proj[2]) * proj[3] * masking)
        .astype(jnp.bfloat16)
        .reshape(hidden_ch, rows, width)
    )
    logits = jnp.dot(gate_weight.T, flat, preferred_element_type=jnp.float32).reshape(
        -1, rows, width
    )
    gate_here = jax.nn.sigmoid(logits)
    tri = jnp.einsum(
        "hik,hjk->hij",
        left,
        lax.all_gather(right, "dap", axis=1, tiled=True),
        preferred_element_type=jnp.float32,
    )
    total, squares = lax.psum((jnp.sum(tri, 0), jnp.sum(tri * tri, 0)), "ch")
    tri_ln = normalize(tri, total, squares, TRI_CH, hid_gain, hid_bias).astype(jnp.bfloat16)
    proj_out = lax.psum_scatter(
        jnp.einsum("ho,hab->oab", out_weight, tri_ln, preferred_element_type=jnp.float32),
        "ch",
        scatter_dimension=0,
        tiled=True,
    )
    update = (gate_here * proj_out).astype(jnp.bfloat16)
    swapped = lax.all_to_all(update, "dap", split_axis=2, concat_axis=1, tiled=True)
    return jnp.swapaxes(swapped, 1, 2)


def solution(mesh):
    placed = (
        P("ch", "dap", None),
        P("dap", None),
        P(),
        P(),
        P(None, None, "ch"),
        P("ch"),
        P("ch"),
        P("ch", None),
        P(None, "ch"),
    )
    return jax.shard_map(
        body, mesh=mesh, in_specs=placed, out_specs=P("ch", "dap", None), check_vma=False
    )
```

profile of v0, /device:TPU:1, one launch (start us, length us, event | category | flops | bytes accessed | tf_op | source)
XLA Modules:
  0.0 443.5 jit_solution(7386165090201808029)
XLA Ops:
  6.5 0.7 dynamic_slice.6
  7.3 0.7 dynamic_slice.7
  8.0 0.9 convert_reduce_fusion
  9.0 51.1 %all-reduce.1 = (f32[8,512]{1,0:T(8,128)S(1)}, f32[8,512]{1,0:T(8,128)S(1)}) all-reduce(f32[8,512]{1,0:T(8,128)S(1)} %get-tuple-element.8, f32[8,512]{1,0:T(8,128)S(1)} %get-tuple-element.7), channel_id=1, replica_groups=mesh['dap'=64,'ch'=8] {'ch'}, use_global_device_ids=true, to_apply=%region_3.0 | all-reduce | flops 8192 | bytes 65536 | tf_op jit(solution)/shard_map/psum | solution.py:25
  60.1 1.7 fusion.6
  61.7 0.0 all-gather.3.cloned.1.call-update
  61.8 0.0 all-gather.5.cloned.1.call-start
  61.8 0.7 convert_element_type.25
  62.6 69.4 %all-gather.3.cloned.1.call-done = bf16[128,8,512]{2,1,0:T(8,128)(2,1)} async-done(((bf16[16,8,512]{2,1,0:T(8,128)(2,1)}), bf16[128,8,512]{2,1,0:T(8,128)(2,1)}) %all-gather.3.cloned.1.call-update) | async-done | bytes 1048592 | tf_op jit(solution)/shard_map/all_gather | solution.py:29
  132.0 1.6 copy.22
  133.6 0.3 fusion.20
  133.9 0.1 slice_multiply_fusion
  134.1 0.2 copy.25
  134.3 0.2 copy.24
  134.4 0.7 fusion.8
  135.1 0.0 reduce-scatter.2.cloned.1.call-start
  135.2 123.1 %all-gather.5.cloned.1.call-done = bf16[16,512,512]{2,1,0:T(8,128)(2,1)} async-done(((bf16[16,8,512]{2,1,0:T(8,128)(2,1)}), bf16[16,512,512]{2,1,0:T(8,128)(2,1)}) %all-gather.5.cloned.1.call-update) | async-done | bytes 8388624 | tf_op jit(solution)/shard_map/all_gather | solution.py:51
  258.3 5.7 %fusion.19 = (f32[8,512]{1,0:T(8,128)S(1)}, f32[8,512]{1,0:T(8,128)S(1)}, f32[16,8,512]{2,1,0:T(8,128)S(1)}) fusion(bf16[16,8,512]{2,1,0:T(8,128)(2,1)S(1)} %get-tuple-element.18, bf16[16,512,512]{2,1,0:T(8,128)(2,1)} %all-gather.5.cloned.1.call-done), kind=kOutput, calls=%fused_computation.37 | convolution fusion | flops 67297280 | bytes 8814592 | tf_op jit(solution)/shard_map/hik,hjk->hij/dot_general | solution.py:48
  263.9 44.8 %all-reduce = (f32[8,512]{1,0:T(8,128)S(1)}, f32[8,512]{1,0:T(8,128)S(1)}) all-reduce(f32[8,512]{1,0:T(8,128)S(1)} %get-tuple-element.6, f32[8,512]{1,0:T(8,128)S(1)} %get-tuple-element.5), channel_id=1, replica_groups=mesh['dap'=64,'ch'=8] {'ch'}, use_global_device_ids=true, to_apply=%region_7.0 | all-reduce | flops 8192 | bytes 65536 | tf_op jit(solution)/shard_map/psum | solution.py:54
  308.8 0.1 add_convert_fusion
  308.9 0.5 convolution_bitcast_fusion
  309.4 2.1 copy.18
  311.5 0.3 fusion.2
  311.7 0.2 copy.23
  311.9 99.2 %reduce-scatter.2.cloned.1.call-done = f32[16,8,512]{2,1,0:T(8,128)} async-done(((f32[128,8,512]{2,1,0:T(8,128)}), f32[16,8,512]{2,1,0:T(8,128)}) %reduce-scatter.2.cloned.1.call-update) | async-done | bytes 262160 | tf_op jit(solution)/shard_map/reduce_scatter | solution.py:56
  411.1 1.0 fusion.10
  412.0 0.8 copy.19
  412.9 1.1 reshape.53
  414.0 20.5 %all_to_all.18 = bf16[64,2,512]{2,1,0:T(2,128)(2,1)S(1)} all-to-all(bf16[64,2,512]{2,1,0:T(2,128)(2,1)S(1)} %reshape.53), channel_id=1, replica_groups=mesh['dap'=64,'ch'=8] {'dap'}, dimensions={0} | all-to-all | bytes 262144 | tf_op jit(solution)/shard_map/all_to_all | solution.py:63
  434.5 0.7 reshape.54
  435.2 0.3 copy.20
  435.5 1.5 copy.21
  (15 shorter events, 0.1 us)
Async XLA Ops:
  6.5 127.1 %copy-start = (bf16[4,128,16]{1,2,0:T(8,128)(2,1)S(1)}, bf16[4,128,16]{1,2,0:T(8,128)(2,1)}, u32[]{:S(2)}) copy-start(bf16[4,128,16]{1,2,0:T(8,128)(2,1)} %param.13) | copy-start | bytes 49156
  6.5 125.5 %all-gather.3.cloned.1.call-start = ((), (), s32[]{:S(2)}) async-start(), calls=%async_computation.2 | async-start | bytes 1179648 | tf_op jit(solution)/shard_map/all_gather | solution.py:29
  61.8 247.0 %copy-start.2 = (f32[16]{0:T(128)S(1)}, f32[16]{0:T(128)}, u32[]{:S(2)}) copy-start(f32[16]{0:T(128)} %param.15) | copy-start | bytes 196
  61.8 247.0 %copy-start.3 = (f32[16]{0:T(128)S(1)}, f32[16]{0:T(128)}, u32[]{:S(2)}) copy-start(f32[16]{0:T(128)} %param.14) | copy-start | bytes 196
  61.8 196.5 %all-gather.5.cloned.1.call-start = ((), (), s32[]{:S(2)}) async-start(), calls=%async_computation.3 | async-start | bytes 8519680 | tf_op jit(solution)/shard_map/all_gather | solution.py:51
  132.0 176.9 %copy-start.1 = (bf16[16,128]{1,0:T(8,128)(2,1)S(1)}, bf16[16,128]{1,0:T(8,128)(2,1)}, u32[]{:S(2)}) copy-start(bf16[16,128]{1,0:T(8,128)(2,1)} %param.16) | copy-start | bytes 12292
  135.1 275.9 %reduce-scatter.2.cloned.1.call-start = ((), (), s32[]{:S(2)}) async-start(), calls=%async_computation.4 | async-start | bytes 2359296 | tf_op jit(solution)/shard_map/reduce_scatter | solution.py:56
  258.3 53.2 %copy-start.4 = (bf16[128,16]{0,1:T(8,128)(2,1)S(1)}, bf16[128,16]{0,1:T(8,128)(2,1)}, u32[]{:S(2)}) copy-start(bf16[128,16]{0,1:T(8,128)(2,1)} %param.17) | copy-start | bytes 12292
Sparse Core Ops, SparseCore 0:
  61.9 70.0 all-gather.2
  135.3 122.9 all-gather.4
  311.6 99.4 reduce-scatter.1
where the time goes:
time: 444 us
  waiting for transfers between devices  292 us (66%)
  blocking collectives  116 us (26%)
  between operations  13.2 us (3%)
  local copies, waits for them, and re-layouts  10.1 us (2%)
  matrix products  6.7 us (2%)
  other arithmetic  5.29 us (1%)
    all_gather x1, waiting for transfers between devices, body(): lax.all_gather(right, 'dap', axis=1, tiled=True)  123 us
    reduce_scatter x1, waiting for transfers between devices, body(): lax.psum_scatter(jnp.einsum('ho,hab->oab', out_weight, tri_ln, preferred_...  99.2 us
    all_gather x1, waiting for transfers between devices, body(): z_ln = lax.all_gather(own_norm, 'ch', axis=0, tiled=True)  69.4 us
    psum x1, blocking collectives, body(): lax.psum((jnp.sum(floats, 0), jnp.sum(floats * floats, 0)), 'ch')  51.1 us
    psum x1, blocking collectives, body(): total, squares = lax.psum((jnp.sum(tri, 0), jnp.sum(tri * tri, 0)), 'ch')  44.8 us
    all_to_all x1, blocking collectives, body(): lax.all_to_all(update, 'dap', split_axis=2, concat_axis=1, tiled=True)  20.5 us
  transfers between devices with their start and end apart: 3, of which 3 were waited for; matrix products, arithmetic and copies ran while one was open for 0% of the time, Pallas kernels for 0%

commit v1 on v0

v1 whole, which is shorter than its diff:
```python
import jax
import jax.numpy as jnp
from jax import lax
from jax.experimental import pallas as pl
from jax.experimental.pallas import tpu as pltpu
from jax.sharding import PartitionSpec as P

CH = 128
RES = 512
EPS = 1e-05
MESH = pl.DeviceIdType.MESH
F32 = jnp.float32
BF16 = jnp.bfloat16


def nt(a, b):
    return lax.dot_general(a, b, (((1,), (1,)), ((), ())), preferred_element_type=F32)


def nn(a, b):
    return lax.dot_general(a, b, (((1,), (0,)), ((), ())), preferred_element_type=F32)


def iota(shape, dim):
    return lax.broadcasted_iota(jnp.int32, shape, dim)


def sigmoid(x):
    return 1.0 / (1.0 + jnp.exp(-x))


def norm(values, gain, bias):
    mean = jnp.sum(values, 0, keepdims=True) * (1.0 / CH)
    square = jnp.sum(values * values, 0, keepdims=True) * (1.0 / CH)
    var = square - mean * mean
    return (values - mean) * lax.rsqrt(var + EPS) * gain + bias


def kernel(pair, mask, gain, bias, ab, hid_gain, hid_bias, out_weight, gate_weight, out,
           work, zsend, zrecv, wasend, warecv, wbsend, wbrecv, hsend, hrecv,
           lrsend, lrrecv, rows, lbuf, rbuf, tsend, t1, t2send, t2, gsend, g1, g2send, g2, usend,
           ssem, rsem):
    dap = lax.axis_index("dap")
    ch = lax.axis_index("ch")
    p = lax.div(dap, 2)
    core = lax.rem(dap, 2)
    q = core * 8 + ch
    y = lax.div(p, 4)
    z = lax.rem(p, 4)
    zh = lax.div(z, 2)
    zl = lax.rem(z, 2)

    def dev_q(q2):
        return (p * 2 + lax.div(q2, 8), lax.rem(q2, 8))

    def dev_p(p2):
        return (p2 * 2 + core, ch)

    def each(first, last, body):
        def step(k, carry):
            body(k)
            return carry
        lax.fori_loop(first, last, step, 0)

    def send(src, dst, sem, device):
        pltpu.make_async_remote_copy(
            src_ref=src, dst_ref=dst, send_sem=ssem.at[sem], recv_sem=rsem.at[sem],
            device_id=device, device_id_type=MESH).start()

    def wait_in(ref, sem):
        pltpu.make_async_copy(ref, ref, rsem.at[sem]).wait()

    def wait_out(ref, sem):
        pltpu.make_async_copy(ref, ref, ssem.at[sem]).wait()

    barrier = pltpu.get_barrier_semaphore()

    def greet_q(k):
        pl.semaphore_signal(barrier, inc=1, device_id=dev_q(lax.rem(q + k, 16)), device_id_type=MESH)

    def greet_p(k):
        pl.semaphore_signal(barrier, inc=1, device_id=dev_p(lax.rem(p + k, 32)), device_id_type=MESH)

    each(1, 16, greet_q)
    each(1, 32, greet_p)

    for kc in range(4):
        lanes = pl.ds(kc * 128, 128)
        work[kc, pl.ds(0, 128), :] = pair[:, :, lanes].astype(F32).reshape(128, 128)
    for kc in range(4):
        lanes = pl.ds(kc * 128, 128)
        for r in range(8):
            zsend[r, :, lanes] = work[kc, pl.ds(r, 16, stride=8), :].astype(BF16)
    eye16 = (iota((16, 16), 0) == iota((16, 16), 1)).astype(BF16)
    for m in range(4):
        wasend[pl.ds(m * 16, 16), :] = nt(eye16, ab[m]).astype(BF16)
    wbsend[pl.ds(0, 16), :] = nt(eye16, gate_weight[...]).astype(BF16)
    wbsend[pl.ds(16, 16), :] = out_weight[...]
    hsend[...] = jnp.zeros((8, 128), F32)
    hsend[pl.ds(0, 1), pl.ds(0, 16)] = hid_gain[...]
    hsend[pl.ds(1, 1), pl.ds(0, 16)] = hid_bias[...]

    pl.semaphore_wait(barrier, 46)

    def peer(k):
        return lax.rem(ch + k, 8)

    each(1, 8, lambda k: send(zsend.at[peer(k)], zrecv.at[ch], 0, (dap, peer(k))))
    each(1, 8, lambda k: send(wasend, warecv.at[ch], 1, (dap, peer(k))))
    each(1, 8, lambda k: send(wbsend, wbrecv.at[ch], 2, (dap, peer(k))))
    each(1, 8, lambda k: send(hsend, hrecv.at[ch], 3, (dap, peer(k))))
    zrecv[ch] = zsend[ch]
    warecv[ch] = wasend[...]
    wbrecv[ch] = wbsend[...]
    hrecv[ch] = hsend[...]

    eye = iota((128, 128), 0) == iota((128, 128), 1)
    gain_col = jnp.sum(jnp.where(eye, gain[...], 0.0), 1, keepdims=True)
    bias_col = jnp.sum(jnp.where(eye, bias[...], 0.0), 1, keepdims=True)
    masking = mask[pl.ds(ch, 1), :].astype(F32)

    wait_in(zrecv.at[pl.ds(0, 7)], 0)
    zn = norm(zrecv[...].astype(F32).reshape(128, RES), gain_col, bias_col).astype(BF16)
    wait_in(warecv.at[pl.ds(0, 7)], 1)

    def project(m):
        weight = warecv[:, pl.ds(m * 16, 16), :].reshape(128, 128)
        return nn(weight, zn)

    left = (sigmoid(project(0)) * project(1) * masking).reshape(16, 8, RES)
    right = (sigmoid(project(2)) * project(3) * masking).reshape(16, 8, RES)
    lrsend[...] = jnp.concatenate([left, right], axis=1).astype(BF16)

    def other_q(k):
        return lax.rem(q + k, 16)

    each(1, 16, lambda k: send(lrsend.at[other_q(k)], lrrecv.at[q], 4, dev_q(other_q(k))))
    lrrecv[q] = lrsend[q]

    wait_in(wbrecv.at[pl.ds(0, 7)], 2)
    gate = sigmoid(nn(wbrecv[:, pl.ds(0, 16), :].reshape(128, 128), zn))
    gsend[...] = gate.T.astype(BF16).reshape(32, 16, 128)

    def other_p(k):
        return lax.rem(p + k, 32)

    each(1, 32, lambda k: send(gsend.at[other_p(k)], g1.at[p], 5, dev_p(other_p(k))))
    g1[p] = gsend[p]
    wout_t = nt(eye.astype(BF16), wbrecv[:, pl.ds(16, 16), :].reshape(128, 128)).astype(BF16)

    wait_in(lrrecv.at[pl.ds(0, 15)], 4)
    for kc in range(4):
        work[kc, :, :] = lrrecv[:, :, pl.ds(kc * 128, 128)].astype(F32).reshape(256, 128)
    for t in range(16):
        for kc in range(4):
            rows[t, :, pl.ds(kc * 128, 128)] = work[kc, pl.ds(t, 16, stride=16), :].astype(BF16)

    lslot = y * 2 + zl
    rslot = y * 2 + zh
    lpair = zh * 2 + (1 - zl)
    rpair = (1 - zh) * 2 + zl

    send(rows.at[y], lbuf.at[lslot], 6, dev_p(y * 4 + lpair))
    send(rows.at[8 + y], rbuf.at[rslot], 11, dev_p(y * 4 + rpair))

    def share(k):
        h = lax.rem(y + k, 8)
        send(rows.at[h], lbuf.at[lslot], 6, dev_p(h * 4 + z))
        send(rows.at[8 + h], rbuf.at[rslot], 11, dev_p(h * 4 + z))
        send(rows.at[h], lbuf.at[lslot], 6, dev_p(h * 4 + lpair))
        send(rows.at[8 + h], rbuf.at[rslot], 11, dev_p(h * 4 + rpair))

    each(1, 8, share)
    lbuf[lslot] = rows[y]
    rbuf[rslot] = rows[8 + y]

    wait_in(g1.at[pl.ds(0, 31)], 5)
    work[0, :, :] = g1[pl.ds(0, 16)].astype(F32).reshape(256, 128)
    work[1, :, :] = g1[pl.ds(16, 16)].astype(F32).reshape(256, 128)
    for j in range(16):
        for half in range(2):
            g2send[j, pl.ds(half * 16, 16), :] = work[half, pl.ds(j, 16, stride=16), :].astype(BF16)
    each(1, 16, lambda k: send(g2send.at[other_q(k)], g2.at[q], 7, dev_q(other_q(k))))
    g2[q] = g2send[q]

    wait_in(lbuf.at[pl.ds(0, 15)], 6)
    wait_in(rbuf.at[pl.ds(0, 15)], 11)
    tri = nt(rbuf[...].reshape(256, RES), lbuf[...].reshape(256, RES))
    tsend[...] = tri.astype(BF16).reshape(16, 16, 256)
    tslot = zh * 8 + y

    def back(k):
        b = lax.rem(rslot + k, 16)
        send(tsend.at[b], t1.at[tslot], 8, dev_p(lax.div(b, 2) * 4 + lax.rem(b, 2) * 2 + zl))

    each(1, 16, back)
    t1[tslot] = tsend[rslot]

    wait_in(t1.at[pl.ds(0, 15)], 8)
    for kc in range(2):
        work[kc, :, :] = t1[:, :, pl.ds(kc * 128, 128)].astype(F32).reshape(256, 128)
    for j in range(16):
        for kc in range(2):
            t2send[j, :, pl.ds(kc * 128, 128)] = work[kc, pl.ds(j, 16, stride=16), :].astype(BF16)
    each(1, 16, lambda k: send(t2send.at[other_q(k)], t2.at[q], 9, dev_q(other_q(k))))
    t2[q] = t2send[q]

    wait_in(g2.at[pl.ds(0, 15)], 7)
    work[2, :, :] = g2[pl.ds(0, 8)].astype(F32).reshape(256, 128)
    work[3, :, :] = g2[pl.ds(8, 8)].astype(F32).reshape(256, 128)
    pieces = []
    for zhi in range(2):
        for yy in range(8):
            for zlo in range(2):
                at = yy * 4 + zhi * 2 + zlo
                pieces.append(work[2, pl.ds(at, 8, stride=32), :])
                pieces.append(work[3, pl.ds(at, 8, stride=32), :])
    gate_t = jnp.concatenate(pieces, axis=0).T
    wait_in(hrecv.at[pl.ds(0, 7)], 3)
    at_lane = (iota((8, 16, 128), 1) == iota((8, 16, 128), 2))
    hg_col = jnp.sum(jnp.where(at_lane, hrecv[:, pl.ds(0, 1), :], 0.0), 2, keepdims=True).reshape(128, 1)
    hb_col = jnp.sum(jnp.where(at_lane, hrecv[:, pl.ds(1, 1), :], 0.0), 2, keepdims=True).reshape(128, 1)
    lane = iota((RES, RES), 0)
    natural = lax.rem(lane, 256) // 32 * 64 + lane // 256 * 32 + lax.rem(lane, 32)
    perm = (natural == iota((RES, RES), 1)).astype(BF16)

    wait_in(t2.at[pl.ds(0, 15)], 9)
    tri = t2[...].astype(F32).reshape(16, 2, 8, 256)
    tri = jnp.concatenate([tri[:, 0].reshape(128, 256), tri[:, 1].reshape(128, 256)], axis=1)
    tri_ln = norm(tri, hg_col, hb_col).astype(BF16)
    update = (nn(wout_t, tri_ln) * gate_t).astype(BF16)
    usend[...] = nn(update, perm).astype(BF16).reshape(8, 16, RES)
    each(1, 8, lambda k: send(usend.at[peer(k)], out.at[ch], 10, (dap, peer(k))))
    out[ch] = usend[ch]

    wait_out(zsend.at[pl.ds(0, 7)], 0)
    wait_out(warecv.at[pl.ds(0, 7)], 1)
    wait_out(wbrecv.at[pl.ds(0, 7)], 2)
    wait_out(hrecv.at[pl.ds(0, 7)], 3)
    wait_out(lrsend.at[pl.ds(0, 15)], 4)
    wait_out(gsend.at[pl.ds(0, 31)], 5)
    wait_out(rows.at[pl.ds(0, 15)], 6)
    wait_out(rows.at[pl.ds(0, 15)], 11)
    wait_out(g2send.at[pl.ds(0, 15)], 7)
    wait_out(tsend.at[pl.ds(0, 15)], 8)
    wait_out(t2send.at[pl.ds(0, 15)], 9)
    wait_out(usend.at[pl.ds(0, 7)], 10)
    wait_in(out.at[pl.ds(0, 7)], 10)


def body(pair, pair_mask, in_gain, in_bias, ab_weight, hid_gain, hid_bias, out_weight, gate_weight):
    vmem = pl.BlockSpec(memory_space=pltpu.VMEM)
    swapped = pl.pallas_call(
        kernel,
        out_shape=jax.ShapeDtypeStruct((8, 16, RES), BF16),
        in_specs=[vmem] * 9,
        out_specs=vmem,
        scratch_shapes=[
            pltpu.VMEM((4, 256, 128), F32),
            pltpu.VMEM((8, 16, RES), BF16),
            pltpu.VMEM((8, 16, RES), BF16),
            pltpu.VMEM((64, 128), BF16),
            pltpu.VMEM((8, 64, 128), BF16),
            pltpu.VMEM((32, 128), BF16),
            pltpu.VMEM((8, 32, 128), BF16),
            pltpu.VMEM((8, 128), F32),
            pltpu.VMEM((8, 8, 128), F32),
            pltpu.VMEM((16, 16, RES), BF16),
            pltpu.VMEM((16, 16, RES), BF16),
            pltpu.VMEM((16, 16, RES), BF16),
            pltpu.VMEM((16, 16, RES), BF16),
            pltpu.VMEM((16, 16, RES), BF16),
            pltpu.VMEM((16, 16, 256), BF16),
            pltpu.VMEM((16, 16, 256), BF16),
            pltpu.VMEM((16, 16, 256), BF16),
            pltpu.VMEM((16, 16, 256), BF16),
            pltpu.VMEM((32, 16, 128), BF16),
            pltpu.VMEM((32, 16, 128), BF16),
            pltpu.VMEM((16, 32, 128), BF16),
            pltpu.VMEM((16, 32, 128), BF16),
            pltpu.VMEM((8, 16, RES), BF16),
            pltpu.SemaphoreType.DMA((12,)),
            pltpu.SemaphoreType.DMA((12,)),
        ],
        compiler_params=pltpu.CompilerParams(
            collective_id=0, has_side_effects=True, vmem_limit_bytes=32 * 1024 * 1024),
    )(pair, pair_mask, in_gain.reshape(1, CH), in_bias.reshape(1, CH), ab_weight,
      hid_gain.reshape(1, 16), hid_bias.reshape(1, 16), out_weight, gate_weight)
    return jnp.swapaxes(swapped, 0, 1)


def solution(mesh):
    placed = (
        P("ch", "dap", None),
        P("dap", None),
        P(),
        P(),
        P(None, None, "ch"),
        P("ch"),
        P("ch"),
        P("ch", None),
        P(None, "ch"),
    )
    return jax.shard_map(
        body, mesh=mesh, in_specs=placed, out_specs=P("ch", "dap", None), check_vma=False
    )
```

time: 444 us -> 75.3 us (0.17)
  waiting for transfers between devices: 292 us -> 0 us
  blocking collectives: 116 us -> 0 us
  Pallas kernels: 0 us -> 71.8 us
  between operations: 13.2 us -> 0.11 us
  local copies, waits for them, and re-layouts: 10.1 us -> 2.45 us
  matrix products: 6.7 us -> 0 us
  other arithmetic: 5.29 us -> 0 us
    all_gather x2 -> x0, waiting for transfers between devices: 193 us -> none  [the longest x1 123 us: body(): lax.all_gather(right, 'dap', axis=1, tiled=True)]
    reduce_scatter x1 -> x0, waiting for transfers between devices: 99.2 us -> none  [body(): lax.psum_scatter(jnp.einsum('ho,hab->oab', out_weight, tri_ln, preferred_...]
    psum x2 -> x0, blocking collectives: 95.9 us -> none  [the longest x1 51.1 us: body(): lax.psum((jnp.sum(floats, 0), jnp.sum(floats * floats, 0)), 'ch')]
    pallas_call x0 -> x1, Pallas kernels: none -> 71.8 us  [body(): pl.pallas_call(kernel, out_shape=jax.ShapeDtypeStruct((8, 16, RES), BF16)...]
    all_to_all x1 -> x0, blocking collectives: 20.5 us -> none  [body(): lax.all_to_all(update, 'dap', split_axis=2, concat_axis=1, tiled=True)]
    dot_general x3 -> x0, matrix products: 6.41 us -> none  [the longest x1 5.66 us: body(): jnp.einsum('hik,hjk->hij', left, lax.all_gather(right, 'dap', axis=1, til...]
  transfers between devices with their start and end apart: 3 -> 0, of which waited for: 3 -> 0; matrix products, arithmetic and copies ran while one was open for 0% -> 0% of each run, Pallas kernels for 0% -> 0%
where the time goes in v1:
time: 75.3 us; the launch traced here: 74.3 us
  Pallas kernels  71.8 us (95%)
  local copies, waits for them, and re-layouts  2.45 us (3%)
    pallas_call x1, Pallas kernels, body(): pl.pallas_call(kernel, out_shape=jax.ShapeDtypeStruct((8, 16, RES), BF16)...  71.8 us
    unnamed x18, local copies, waits for them, and re-layouts  1.72 us

profile of v1, /device:TPU:1, one launch (start us, length us, event | category | flops | bytes accessed | tf_op | source)
XLA Modules:
  0.0 74.3 jit_solution(16606574622163773960)
XLA Ops:
  0.0 0.0 copy-start.7
  0.0 0.0 copy-start
  0.0 0.7 copy-done.7
  0.7 0.1 copy.11.gate_weight
  0.8 0.0 copy-start.1
  0.8 0.0 copy-start.2
  0.8 0.0 copy-start.3
  0.8 0.0 copy-start.4
  0.9 0.0 copy-start.5
  0.9 0.0 copy-start.6
  0.9 0.9 %copy.10.ab = bf16[4,128,16]{2,1,0:T(8,128)(2,1)S(1)} copy(bf16[4,128,16]{1,2,0:T(8,128)(2,1)} %param.13) | data formatting | bytes 32768 | tf_op args[4]
  1.7 0.0 copy-done
  1.8 0.0 copy-done.1
  1.8 0.0 copy-done.2
  1.8 0.0 copy-done.3
  1.8 0.0 copy-done.4
  1.8 0.0 copy-done.5
  1.8 0.0 copy-done.6
  1.8 71.8 %shard_map.91 = bf16[8,16,512]{2,1,0:T(8,128)(2,1)S(1)} custom-call(bf16[16,8,512]{2,1,0:T(8,128)(2,1)S(1)} %copy-done, s32[8,512]{1,0:T(8,128)S(1)} %copy-done.1, f32[1,128]{1,0:T(1,128)S(1)} %bitcast.6, f32[1,128]{1,0:T(1,128)S(1)} %bitcast.7, bf16[4,128,16]{2,1,0:T(8,128)(2,1)S(1)} %copy.10.ab, f32[1,16]{1,0:T(1,128)S(1)} %bitcast.8, ...), custom_call_target="tpu_custom_call" | custom-call | tf_op jit(solution)/shard_map/pallas_call | solution.py:253
  73.6 0.7 copy.12
Async XLA Ops:
  0.0 0.7 copy-start.7
  0.0 1.7 %copy-start = (bf16[16,8,512]{2,1,0:T(8,128)(2,1)S(1)}, bf16[16,8,512]{2,1,0:T(8,128)(2,1)}, u32[]{:S(2)}) copy-start(bf16[16,8,512]{2,1,0:T(8,128)(2,1)} %pair.1) | copy-start | bytes 393220
  0.8 1.0 %copy-start.1 = (s32[8,512]{1,0:T(8,128)S(1)}, s32[8,512]{1,0:T(8,128)}, u32[]{:S(2)}) copy-start(s32[8,512]{1,0:T(8,128)} %mask.1) | copy-start | bytes 49156
  0.8 1.0 %copy-start.2 = (bf16[16,128]{1,0:T(8,128)(2,1)S(1)}, bf16[16,128]{1,0:T(8,128)(2,1)}, u32[]{:S(2)}) copy-start(bf16[16,128]{1,0:T(8,128)(2,1)} %out_weight.1) | copy-start | bytes 12292
  0.8 1.0 %copy-start.3 = (f32[128]{0:T(128)S(1)}, f32[128]{0:T(128)}, u32[]{:S(2)}) copy-start(f32[128]{0:T(128)} %param.11) | copy-start | bytes 1540
  0.8 1.0 %copy-start.4 = (f32[128]{0:T(128)S(1)}, f32[128]{0:T(128)}, u32[]{:S(2)}) copy-start(f32[128]{0:T(128)} %param.12) | copy-start | bytes 1540
  0.9 1.0 %copy-start.5 = (f32[16]{0:T(128)S(1)}, f32[16]{0:T(128)}, u32[]{:S(2)}) copy-start(f32[16]{0:T(128)} %param.14) | copy-start | bytes 196
  0.9 0.9 %copy-start.6 = (f32[16]{0:T(128)S(1)}, f32[16]{0:T(128)}, u32[]{:S(2)}) copy-start(f32[16]{0:T(128)} %param.15) | copy-start | bytes 196

commit v2 on v0

v2 whole, which is shorter than its diff:
```python
import jax
import jax.numpy as jnp
from jax import lax
from jax.experimental import pallas as pl
from jax.experimental.pallas import tpu as pltpu
from jax.sharding import PartitionSpec as P

CH = 128
RES = 512
EPS = 1e-05
MESH = pl.DeviceIdType.MESH
F32 = jnp.float32
BF16 = jnp.bfloat16


def nt(a, b):
    return lax.dot_general(a, b, (((1,), (1,)), ((), ())), preferred_element_type=F32)


def nn(a, b):
    return lax.dot_general(a, b, (((1,), (0,)), ((), ())), preferred_element_type=F32)


def iota(shape, dim):
    return lax.broadcasted_iota(jnp.int32, shape, dim)


def bits(value, low, count):
    return lax.shift_right_logical(value, low) & ((1 << count) - 1)


def sigmoid(x):
    return 1.0 / (1.0 + jnp.exp(-x))


def norm(values, gain, bias):
    mean = jnp.sum(values, 0, keepdims=True) * (1.0 / CH)
    square = jnp.sum(values * values, 0, keepdims=True) * (1.0 / CH)
    var = square - mean * mean
    return (values - mean) * lax.rsqrt(var + EPS) * gain + bias


def each(first, last, body):
    def step(k, carry):
        body(k)
        return carry
    lax.fori_loop(first, last, step, 0)


def kernel(pair, mask, gain, bias, ab, hid_gain, hid_bias, out_weight, gate_weight, out,
           work, zsend, zrecv, wasend, warecv, wbsend, wbrecv, hsend, hrecv, msend, mrecv,
           lrsend, lrrecv, rows, lbuf, rbuf, tsend, t1, t2send, t2, gsend, g1, g2send, g2, usend,
           ssem, rsem):
    div, rem = lax.div, lax.rem
    dap = lax.axis_index("dap")
    ch = lax.axis_index("ch")
    x, z_hi = div(ch, 2), rem(ch, 2)
    y, z_lo, core = div(dap, 8), rem(div(dap, 2), 4), rem(dap, 2)
    z = z_hi * 4 + z_lo
    b = y * 2 + core
    e_lo, e_ch = rem(z + 2, 4), 2 * x + div(rem(z + 6, 8), 4)
    e = e_lo * 8 + e_ch
    half, quarter = div(y, 4), rem(y, 4)

    def place(x2, z2):
        return ((y * 4 + rem(z2, 4)) * 2 + core, x2 * 2 + div(z2, 4))

    def dev_e(e2):
        return place(div(rem(e2, 8), 2), rem(div(e2, 8) + 2 + 4 * rem(e2, 2), 8))

    def dev_b(b2):
        return ((div(b2, 2) * 4 + z_lo) * 2 + rem(b2, 2), ch)

    def send(src, dst, sem, device):
        pltpu.make_async_remote_copy(
            src_ref=src, dst_ref=dst, send_sem=ssem.at[sem], recv_sem=rsem.at[sem],
            device_id=device, device_id_type=MESH).start()

    def wait_in(ref, sem):
        pltpu.make_async_copy(ref, ref, rsem.at[sem]).wait()

    def wait_out(ref, sem):
        pltpu.make_async_copy(ref, ref, ssem.at[sem]).wait()

    barrier = pltpu.get_barrier_semaphore()

    def greet(device):
        pl.semaphore_signal(barrier, inc=1, device_id=device, device_id_type=MESH)

    def greet_near(k):
        greet(place(rem(x + div(k, 5), 4), rem(z + 6 + rem(k + 2, 5), 8)))

    each(1, 16, lambda k: greet(dev_b(rem(b + k, 16))))
    each(1, 20, greet_near)

    for kc in range(4):
        work[kc, pl.ds(0, 128), :] = pair[:, :, pl.ds(kc * 128, 128)].astype(F32).reshape(128, 128)
    for kc in range(4):
        for r in range(8):
            zsend[r, :, pl.ds(kc * 128, 128)] = work[kc, pl.ds(r, 16, stride=8), :].astype(BF16)
    own_mask = mask[pl.ds(ch, 1), :].astype(F32)
    for kc in range(4):
        msend[pl.ds(kc, 1), :] = own_mask[:, kc * 128:kc * 128 + 128]

    pl.semaphore_wait(barrier, 34)

    each(0, 8, lambda k: send(zsend.at[rem(ch + k, 8)], zrecv.at[ch], 0, dev_e(z_lo * 8 + rem(ch + k, 8))))
    send(msend, mrecv, 13, dev_e(z_lo * 8 + ch))

    at = iota((64, 64), 0)
    source = bits(at, 2, 1) * 32 + bits(at, 5, 1) * 16 + bits(at, 3, 2) * 4 + bits(at, 0, 2)
    order = (source == iota((64, 64), 1)).astype(BF16)
    wasend[...] = nn(order, ab[...].reshape(64, 128)).astype(BF16)
    z6 = 4 * (1 - z_hi) + 2 * (1 - div(z_lo, 2)) + rem(z_lo, 2)

    def spread(src, dst, sem):
        each(0, 4, lambda k: send(src, dst, sem, place(rem(x + k, 4), z6)))
        each(1, 4, lambda k: send(src, dst, sem, place(rem(x + k, 4), z)))

    spread(wasend, warecv.at[ch], 1)
    wbsend[pl.ds(0, 16), :] = gate_weight[...]
    wbsend[pl.ds(16, 16), :] = out_weight[...]
    hsend[...] = jnp.zeros((8, 128), F32)
    hsend[pl.ds(0, 1), pl.ds(0, 16)] = hid_gain[...]
    hsend[pl.ds(1, 1), pl.ds(0, 16)] = hid_bias[...]
    spread(wbsend, wbrecv.at[ch], 2)
    spread(hsend, hrecv.at[ch], 3)
    warecv[ch] = wasend[...]
    wbrecv[ch] = wbsend[...]
    hrecv[ch] = hsend[...]

    eye = iota((128, 128), 0) == iota((128, 128), 1)
    gain_col = jnp.sum(jnp.where(eye, gain[...], 0.0), 1, keepdims=True)
    bias_col = jnp.sum(jnp.where(eye, bias[...], 0.0), 1, keepdims=True)

    wait_in(zrecv, 0)
    zn = norm(zrecv[...].astype(F32).reshape(128, RES), gain_col, bias_col).astype(BF16)
    wait_in(mrecv, 13)
    masking = jnp.concatenate([mrecv[pl.ds(kc, 1), :] for kc in range(4)], axis=1)
    wait_in(warecv.at[pl.ds(0, 7)], 1)
    opened = sigmoid(nn(warecv[:, pl.ds(0, 32), :].reshape(256, 128), zn))
    value = nn(warecv[:, pl.ds(32, 32), :].reshape(256, 128), zn)
    both = (opened * value * masking).reshape(32, 8, RES)
    lrsend[...] = jnp.concatenate([both[:, :, :256], both[:, :, 256:]], axis=1).astype(BF16)

    def other_e(k):
        return rem(e + k, 32)

    def other_b(k):
        return rem(b + k, 16)

    each(1, 32, lambda k: send(lrsend.at[other_e(k)], lrrecv.at[e], 4, dev_e(other_e(k))))
    lrrecv[e] = lrsend[e]

    wait_in(wbrecv.at[pl.ds(0, 7)], 2)
    gate = sigmoid(nn(wbrecv[:, pl.ds(0, 16), :].reshape(128, 128), zn)).T.reshape(8, 4, 2, 8, 128)
    for yy in range(8):
        for cc in range(2):
            gsend[yy * 2 + cc] = gate[yy, :, cc].reshape(32, 128).astype(BF16)
    each(1, 16, lambda k: send(gsend.at[other_b(k)], g1.at[b], 5, dev_b(other_b(k))))
    g1[b] = gsend[b]

    wait_in(lrrecv.at[pl.ds(0, 31)], 4)
    for lc in range(2):
        work[lc, :, :] = lrrecv[:, :, pl.ds(lc * 128, 128)].astype(F32).reshape(512, 128)
    for t in range(8):
        for kh in range(2):
            for lc in range(2):
                rows[t, :, pl.ds(kh * 256 + lc * 128, 128)] = work[lc, pl.ds(kh * 8 + t, 32, stride=16), :].astype(BF16)

    def share(k):
        h = rem(quarter + k, 4)
        send(rows.at[h], lbuf.at[quarter, core], 6, dev_b((half * 4 + h) * 2 + core))
        send(rows.at[4 + h], rbuf.at[y], 11, dev_b((half * 4 + h) * 2 + core))
        send(rows.at[4 + h], rbuf.at[y], 11, dev_b(((1 - half) * 4 + h) * 2 + core))

    each(1, 4, share)
    send(rows.at[4 + quarter], rbuf.at[y], 11, dev_b(((1 - half) * 4 + quarter) * 2 + core))
    lbuf[quarter, core] = rows[quarter]
    rbuf[y] = rows[4 + quarter]

    wait_in(g1.at[pl.ds(0, 15)], 5)
    work[2, :, :] = g1[...].astype(F32).reshape(512, 128)
    for j in range(32):
        g2send[j] = work[2, pl.ds(j, 16, stride=32), :].astype(BF16)
    each(1, 32, lambda k: send(g2send.at[other_e(k)], g2.at[e], 7, dev_e(other_e(k))))
    g2[e] = g2send[e]

    wait_in(rbuf.at[pl.ds(0, 3)], 6)
    send(lbuf.at[:, core], lbuf.at[:, core], 12, dev_b(y * 2 + 1 - core))

    def by_block(where, values):
        work[where, pl.ds(0, 128), :] = values
        return jnp.concatenate([work[where, pl.ds(h, 32, stride=4), :] for h in range(4)], axis=0)

    w_out = by_block(3, wbrecv[:, pl.ds(16, 16), :].astype(F32).reshape(128, 128))
    wout_t = nt(eye.astype(BF16), w_out.astype(BF16)).astype(BF16)
    wait_in(hrecv.at[pl.ds(0, 7)], 3)
    at_lane = iota((8, 16, 128), 1) == iota((8, 16, 128), 2)

    def column(row):
        col = jnp.sum(jnp.where(at_lane, hrecv[:, pl.ds(row, 1), :], 0.0), 2, keepdims=True)
        return by_block(3, jnp.broadcast_to(col, (8, 16, 128)).reshape(128, 128))

    hg, hb = column(0), column(1)
    lane = iota((128, 128), 0)
    natural = bits(lane, 6, 1) * 64 + bits(lane, 3, 2) * 16 + bits(lane, 5, 1) * 8 + bits(lane, 0, 3)
    perm = (natural == iota((128, 128), 1)).astype(BF16)

    wait_in(rbuf.at[pl.ds(0, 7)], 11)
    wait_in(rbuf.at[pl.ds(0, 4)], 12)
    tri = nt(rbuf[...].reshape(256, RES), lbuf[...].reshape(256, RES))
    tsend[...] = tri.astype(BF16).reshape(8, 32, 256)

    def back(k):
        y2 = rem(y + k, 8)
        send(tsend.at[y2], t1.at[y], 8, dev_b(y2 * 2 + core))

    each(1, 8, back)
    t1[y] = tsend[y]

    wait_in(g2.at[pl.ds(0, 31)], 7)
    work[2, :, :] = g2[...].astype(F32).reshape(512, 128)
    gate_t = jnp.concatenate([work[2, pl.ds(bb, 32, stride=16), :] for bb in range(16)], axis=0).T

    wait_in(t1.at[pl.ds(0, 7)], 8)
    for lc in range(2):
        work[lc, pl.ds(0, 256), :] = t1[:, :, pl.ds(lc * 128, 128)].astype(F32).reshape(256, 128)
    for j in range(32):
        t2send[j] = jnp.concatenate([work[lc, pl.ds(j, 8, stride=32), :] for lc in range(2)], axis=0).astype(BF16)
    each(1, 32, lambda k: send(t2send.at[other_e(k)], t2.at[e], 9, dev_e(other_e(k))))
    t2[e] = t2send[e]

    wait_in(t2.at[pl.ds(0, 31)], 9)
    work[0, :, :] = t2[...].astype(F32).reshape(512, 128)
    for tile in range(4):
        first = (tile % 2) * 8 + (tile // 2) * 4
        tri = jnp.concatenate([work[0, pl.ds(first + h, 32, stride=16), :] for h in range(4)], axis=0)
        tri_ln = norm(tri, hg, hb).astype(BF16)
        update = (nn(wout_t, tri_ln) * gate_t[:, tile * 128:tile * 128 + 128]).astype(BF16)
        usend[:, :, pl.ds(tile * 128, 128)] = nn(update, perm).astype(BF16).reshape(8, 16, 128)
    home = (y * 4 + e_lo) * 2 + core
    each(0, 8, lambda k: send(usend.at[rem(ch + k, 8)], out.at[e_ch], 10, (home, rem(ch + k, 8))))

    wait_out(zsend, 0)
    wait_out(warecv.at[pl.ds(0, 7)], 1)
    wait_out(wbrecv.at[pl.ds(0, 7)], 2)
    wait_out(hrecv.at[pl.ds(0, 7)], 3)
    wait_out(lrsend.at[pl.ds(0, 31)], 4)
    wait_out(gsend.at[pl.ds(0, 15)], 5)
    wait_out(rows.at[pl.ds(0, 3)], 6)
    wait_out(g2send.at[pl.ds(0, 31)], 7)
    wait_out(tsend.at[pl.ds(0, 7)], 8)
    wait_out(t2send.at[pl.ds(0, 31)], 9)
    wait_out(rows.at[pl.ds(0, 7)], 11)
    wait_out(rows.at[pl.ds(0, 4)], 12)
    wait_out(msend, 13)
    wait_out(usend, 10)
    wait_in(out, 10)


def body(pair, pair_mask, in_gain, in_bias, ab_weight, hid_gain, hid_bias, out_weight, gate_weight):
    vmem = pl.BlockSpec(memory_space=pltpu.VMEM)
    scratch = [
        ((4, 512, 128), F32),
        ((8, 16, RES), BF16), ((8, 16, RES), BF16),
        ((64, 128), BF16), ((8, 64, 128), BF16),
        ((32, 128), BF16), ((8, 32, 128), BF16),
        ((8, 128), F32), ((8, 8, 128), F32),
        ((8, 128), F32), ((8, 128), F32),
        ((32, 16, 256), BF16), ((32, 16, 256), BF16),
        ((8, 32, RES), BF16), ((4, 2, 32, RES), BF16), ((8, 32, RES), BF16),
        ((8, 32, 256), BF16), ((8, 32, 256), BF16),
        ((32, 16, 128), BF16), ((32, 16, 128), BF16),
        ((16, 32, 128), BF16), ((16, 32, 128), BF16),
        ((32, 16, 128), BF16), ((32, 16, 128), BF16),
        ((8, 16, RES), BF16),
    ]
    swapped = pl.pallas_call(
        kernel,
        out_shape=jax.ShapeDtypeStruct((8, 16, RES), BF16),
        in_specs=[vmem] * 9,
        out_specs=vmem,
        scratch_shapes=[pltpu.VMEM(shape, kind) for shape, kind in scratch]
        + [pltpu.SemaphoreType.DMA((14,)), pltpu.SemaphoreType.DMA((14,))],
        compiler_params=pltpu.CompilerParams(
            collective_id=0, has_side_effects=True, vmem_limit_bytes=32 * 1024 * 1024),
    )(pair, pair_mask, in_gain.reshape(1, CH), in_bias.reshape(1, CH), jnp.swapaxes(ab_weight, 1, 2),
      hid_gain.reshape(1, 16), hid_bias.reshape(1, 16), out_weight, gate_weight.T)
    return jnp.swapaxes(swapped, 0, 1)


def solution(mesh):
    placed = (
        P("ch", "dap", None),
        P("dap", None),
        P(),
        P(),
        P(None, None, "ch"),
        P("ch"),
        P("ch"),
        P("ch", None),
        P(None, "ch"),
    )
    return jax.shard_map(
        body, mesh=mesh, in_specs=placed, out_specs=P("ch", "dap", None), check_vma=False
    )
```

time: 444 us -> 68.5 us (0.15)
  waiting for transfers between devices: 292 us -> 0 us
  blocking collectives: 116 us -> 0 us
  Pallas kernels: 0 us -> 63.6 us
  between operations: 13.2 us -> 0.04 us
  matrix products: 6.7 us -> 0 us
  local copies, waits for them, and re-layouts: 10.1 us -> 3.78 us
  other arithmetic: 5.29 us -> 0 us
    all_gather x2 -> x0, waiting for transfers between devices: 193 us -> none  [the longest x1 123 us: body(): lax.all_gather(right, 'dap', axis=1, tiled=True)]
    reduce_scatter x1 -> x0, waiting for transfers between devices: 99.2 us -> none  [body(): lax.psum_scatter(jnp.einsum('ho,hab->oab', out_weight, tri_ln, preferred_...]
    psum x2 -> x0, blocking collectives: 95.9 us -> none  [the longest x1 51.1 us: body(): lax.psum((jnp.sum(floats, 0), jnp.sum(floats * floats, 0)), 'ch')]
    pallas_call x0 -> x1, Pallas kernels: none -> 63.6 us  [body(): pl.pallas_call(kernel, out_shape=jax.ShapeDtypeStruct((8, 16, RES), BF16)...]
    all_to_all x1 -> x0, blocking collectives: 20.5 us -> none  [body(): lax.all_to_all(update, 'dap', split_axis=2, concat_axis=1, tiled=True)]
    dot_general x3 -> x0, matrix products: 6.41 us -> none  [the longest x1 5.66 us: body(): jnp.einsum('hik,hjk->hij', left, lax.all_gather(right, 'dap', axis=1, til...]
  transfers between devices with their start and end apart: 3 -> 0, of which waited for: 3 -> 0; matrix products, arithmetic and copies ran while one was open for 0% -> 0% of each run, Pallas kernels for 0% -> 0%
where the time goes in v2:
time: 68.5 us; the launch traced here: 67.4 us
  Pallas kernels  63.6 us (93%)
  local copies, waits for them, and re-layouts  3.78 us (6%)
    pallas_call x1, Pallas kernels, body(): pl.pallas_call(kernel, out_shape=jax.ShapeDtypeStruct((8, 16, RES), BF16)...  63.6 us
    unnamed x18, local copies, waits for them, and re-layouts  3.05 us

profile of v2, /device:TPU:1, one launch (start us, length us, event | category | flops | bytes accessed | tf_op | source)
XLA Modules:
  0.0 67.4 jit_solution(17686658944401922787)
XLA Ops:
  0.0 0.0 copy-start.7
  0.0 0.0 copy-start.8
  0.0 0.0 copy-start.4
  0.0 0.0 copy-start.3
  0.0 0.0 copy-start.5
  0.0 0.0 copy-start.6
  0.0 0.6 copy-done.7
  0.7 0.0 copy-done.8
  0.7 0.0 copy-done.4
  0.7 0.0 copy-done.3
  0.7 0.0 copy-done.5
  0.7 0.0 copy-done.6
  0.7 0.0 copy-start
  0.7 0.9 %copy-done = bf16[16,8,512]{2,1,0:T(8,128)(2,1)S(1)} copy-done((bf16[16,8,512]{2,1,0:T(8,128)(2,1)S(1)}, bf16[16,8,512]{2,1,0:T(8,128)(2,1)}, u32[]{:S(2)}) %copy-start) | copy-done | bytes 131096
  1.6 0.0 copy-start.1
  1.6 0.7 %copy-done.1 = s32[8,512]{1,0:T(8,128)S(1)} copy-done((s32[8,512]{1,0:T(8,128)S(1)}, s32[8,512]{1,0:T(8,128)}, u32[]{:S(2)}) %copy-start.1) | copy-done | bytes 16408
  2.4 0.0 copy-start.2
  2.4 0.7 %copy-done.2 = bf16[4,128,16]{1,2,0:T(8,128)(2,1)S(1)} copy-done((bf16[4,128,16]{1,2,0:T(8,128)(2,1)S(1)}, bf16[4,128,16]{1,2,0:T(8,128)(2,1)}, u32[]{:S(2)}) %copy-start.2) | copy-done | bytes 16408
  3.1 63.6 %shard_map.91 = bf16[8,16,512]{2,1,0:T(8,128)(2,1)S(1)} custom-call(bf16[16,8,512]{2,1,0:T(8,128)(2,1)S(1)} %copy-done, s32[8,512]{1,0:T(8,128)S(1)} %copy-done.1, f32[1,128]{1,0:T(1,128)S(1)} %bitcast.10, f32[1,128]{1,0:T(1,128)S(1)} %bitcast.11, bf16[4,16,128]{2,1,0:T(8,128)(2,1)S(1)} %bitcast.8, f32[1,16]{1,0:T(1,128)S(1)} %bitcast.12, ...), custom_call_target="tpu_custom_call" | custom-call | tf_op jit(solution)/shard_map/pallas_call | solution.py:279
  66.7 0.7 %copy.10 = bf16[16,8,512]{2,1,0:T(8,128)(2,1)} copy(bf16[16,8,512]{2,0,1:T(8,128)(2,1)S(1)} %bitcast.7) | data formatting | bytes 262144 | tf_op jit(solution)/shard_map/transpose | solution.py:290
Async XLA Ops:
  0.0 0.7 copy-start.7
  0.0 0.7 copy-start.8
  0.0 0.7 %copy-start.4 = (bf16[128,16]{0,1:T(8,128)(2,1)S(1)}, bf16[128,16]{0,1:T(8,128)(2,1)}, u32[]{:S(2)}) copy-start(bf16[128,16]{0,1:T(8,128)(2,1)} %param.17) | copy-start | bytes 12292
  0.0 0.7 %copy-start.3 = (bf16[16,128]{1,0:T(8,128)(2,1)S(1)}, bf16[16,128]{1,0:T(8,128)(2,1)}, u32[]{:S(2)}) copy-start(bf16[16,128]{1,0:T(8,128)(2,1)} %out_weight.1) | copy-start | bytes 12292
  0.0 0.7 %copy-start.5 = (f32[128]{0:T(128)S(1)}, f32[128]{0:T(128)}, u32[]{:S(2)}) copy-start(f32[128]{0:T(128)} %param.11) | copy-start | bytes 1540
  0.0 0.7 %copy-start.6 = (f32[128]{0:T(128)S(1)}, f32[128]{0:T(128)}, u32[]{:S(2)}) copy-start(f32[128]{0:T(128)} %param.12) | copy-start | bytes 1540
  0.7 0.9 %copy-start = (bf16[16,8,512]{2,1,0:T(8,128)(2,1)S(1)}, bf16[16,8,512]{2,1,0:T(8,128)(2,1)}, u32[]{:S(2)}) copy-start(bf16[16,8,512]{2,1,0:T(8,128)(2,1)} %pair.1) | copy-start | bytes 393220
  1.6 0.7 %copy-start.1 = (s32[8,512]{1,0:T(8,128)S(1)}, s32[8,512]{1,0:T(8,128)}, u32[]{:S(2)}) copy-start(s32[8,512]{1,0:T(8,128)} %mask.1) | copy-start | bytes 49156
  2.4 0.7 %copy-start.2 = (bf16[4,128,16]{1,2,0:T(8,128)(2,1)S(1)}, bf16[4,128,16]{1,2,0:T(8,128)(2,1)}, u32[]{:S(2)}) copy-start(bf16[4,128,16]{1,2,0:T(8,128)(2,1)} %param.13) | copy-start | bytes 49156

commit v3 on v2

v3 whole, which is shorter than its diff:
```python
import jax
import jax.numpy as jnp
from jax import lax
from jax.experimental import pallas as pl
from jax.experimental.pallas import tpu as pltpu
from jax.sharding import PartitionSpec as P

CH = 128
RES = 512
EPS = 1e-05
VMEM_LIMIT = 62 * 1024 * 1024
MESH = pl.DeviceIdType.MESH
F32 = jnp.float32
BF16 = jnp.bfloat16


def nt(a, b):
    return lax.dot_general(a, b, (((1,), (1,)), ((), ())), preferred_element_type=F32)


def nn(a, b):
    return lax.dot_general(a, b, (((1,), (0,)), ((), ())), preferred_element_type=F32)


def iota(shape, dim):
    return lax.broadcasted_iota(jnp.int32, shape, dim)


def bits(value, low, count):
    return lax.shift_right_logical(value, low) & ((1 << count) - 1)


def sigmoid(x):
    return 1.0 / (1.0 + jnp.exp(-x))


def norm(values, gain, bias):
    mean = jnp.sum(values, 0, keepdims=True) * (1.0 / CH)
    square = jnp.sum(values * values, 0, keepdims=True) * (1.0 / CH)
    var = square - mean * mean
    return (values - mean) * lax.rsqrt(var + EPS) * gain + bias


def each(first, last, body):
    def step(k, carry):
        body(k)
        return carry
    lax.fori_loop(first, last, step, 0)


def far(n, top):
    return top + lax.div(n + 1, 2) * (1 - 2 * lax.rem(n, 2))


def kernel(pair_in, mask_in, ab_in, gain_in, bias_in, gate_in, out_in, hid_gain_in, hid_bias_in, out,
           pair, mask, wasend, gain, bias, wbsend, hid_gain, hid_bias,
           work, zsend, zrecv, warecv, wbrecv, hsend, hrecv, msend, mrecv,
           rsend, rrecv, lsend, lrecv, rrows, lrows, lbuf, rbuf, tsend, t1, t2send, t2, gsend, g1, g2send, g2, usend,
           lsem, ssem, rsem):
    div, rem = lax.div, lax.rem
    dap = lax.axis_index("dap")
    ch = lax.axis_index("ch")
    x, z_hi = div(ch, 2), rem(ch, 2)
    y, z_lo, core = div(dap, 8), rem(div(dap, 2), 4), rem(dap, 2)
    z = z_hi * 4 + z_lo
    b = y * 2 + core
    e_lo, s = rem(z + 2, 4), div(rem(z + 6, 8), 4)
    e_ch = 2 * x + s
    u = rem(x, 2)
    f = e_lo * 4 + div(x, 2) * 2 + s
    e = u * 16 + f

    def place(x2, z2):
        return ((y * 4 + rem(z2, 4)) * 2 + core, x2 * 2 + div(z2, 4))

    def f_of(x2, z2):
        return rem(z2 + 2, 4) * 4 + div(x2, 2) * 2 + div(rem(z2 + 6, 8), 4)

    def dev_y(y2):
        return ((y2 * 4 + z_lo) * 2 + core, ch)

    sibling = (dap + 1 - 2 * core, ch)

    def send(src, dst, sem, device):
        pltpu.make_async_remote_copy(
            src_ref=src, dst_ref=dst, send_sem=ssem.at[sem], recv_sem=rsem.at[sem],
            device_id=device, device_id_type=MESH).start()

    def wait_in(ref, sem):
        pltpu.make_async_copy(ref, ref, rsem.at[sem]).wait()

    def wait_out(ref, sem):
        pltpu.make_async_copy(ref, ref, ssem.at[sem]).wait()

    def to_x(k):
        return rem(x + far(k, 2), 4)

    def to_y(k):
        return rem(y + far(k, 4), 8)

    def to_z(k):
        return rem(z + far(k, 4), 8)

    loads = [
        pltpu.make_async_copy(source, target, lsem.at[i]) for i, (source, target) in enumerate((
            (pair_in, pair), (mask_in, mask), (ab_in, wasend), (gate_in, wbsend.at[0]), (out_in, wbsend.at[1]),
            (gain_in, gain), (bias_in, bias), (hid_gain_in, hid_gain), (hid_bias_in, hid_bias)))
    ]
    for load in loads:
        load.start()

    barrier = pltpu.get_barrier_semaphore()

    def greet(device):
        pl.semaphore_signal(barrier, inc=1, device_id=device, device_id_type=MESH)

    def greet_y(k):
        y2 = to_y(div(k, 2))
        greet(((y2 * 4 + z_lo) * 2 + rem(core + 1 + k, 2), ch))

    each(0, 15, greet_y)
    each(0, 19, lambda k: greet(place(to_x(div(k, 5)), to_z(rem(k, 5) + 3))))

    for load in loads:
        load.wait()
    for kc in range(4):
        work[kc, pl.ds(0, 128), :] = pair[:, :, pl.ds(kc * 128, 128)].astype(F32).reshape(128, 128)
    for kc in range(4):
        for r in range(8):
            zsend[r, :, pl.ds(kc * 128, 128)] = work[kc, pl.ds(r, 16, stride=8), :].astype(BF16)
    own_mask = mask[pl.ds(ch, 1), :].astype(F32)
    for kc in range(4):
        msend[pl.ds(kc, 1), :] = own_mask[:, kc * 128:kc * 128 + 128]

    pl.semaphore_wait(barrier, 34)

    def first(k):
        x2, s2 = to_x(div(k, 2)), rem(s + k, 2)
        send(zsend.at[x2 * 2 + s2], zrecv.at[ch], 0, place(x2, rem(z_lo + 2 + 4 * s2, 8)))

    each(0, 8, first)
    send(msend, mrecv, 13, place(x, rem(z_lo + 2 + 4 * z_hi, 8)))

    z6 = 4 * (1 - z_hi) + 2 * (1 - div(z_lo, 2)) + rem(z_lo, 2)

    def spread(src, dst, sem):
        each(0, 4, lambda k: send(src, dst, sem, place(to_x(k), z6)))
        each(0, 3, lambda k: send(src, dst, sem, place(to_x(k), z)))

    spread(wasend.at[core], warecv.at[ch, core], 1)
    warecv[ch, core] = wasend[core]

    eye = iota((128, 128), 0) == iota((128, 128), 1)
    gain_col = jnp.sum(jnp.where(eye, gain[...], 0.0), 1, keepdims=True)
    bias_col = jnp.sum(jnp.where(eye, bias[...], 0.0), 1, keepdims=True)
    hsend[...] = jnp.zeros((1, 128), F32)
    hsend[:, pl.ds(0, 16)] = hid_gain[...]
    hsend[:, pl.ds(16, 16)] = hid_bias[...]

    wait_in(warecv.at[pl.ds(0, 7), 0], 1)
    send(warecv.at[:, core], warecv.at[:, core], 2, sibling)
    wait_in(zrecv, 0)
    zn = norm(zrecv[...].astype(F32).reshape(128, RES), gain_col, bias_col).astype(BF16)
    wait_in(mrecv, 13)
    masking = jnp.concatenate([mrecv[pl.ds(kc, 1), :] for kc in range(4)], axis=1)
    wait_in(warecv.at[:, 0], 2)

    def operand(side):
        weight = warecv[:, side]
        opened = sigmoid(nn(weight[:, :16].reshape(128, 128), zn))
        value = nn(weight[:, 16:].reshape(128, 128), zn)
        full = (opened * value * masking).reshape(16, 8, RES)
        return jnp.concatenate([full[:, :, :256], full[:, :, 256:]], axis=1).astype(BF16)

    def swap_f(sent, received, sem):
        def one(k):
            x2, z2 = rem(x + 2 * rem(k + 1, 2), 4), to_z(div(k, 2))
            send(sent.at[f_of(x2, z2)], received.at[f], sem, place(x2, z2))
        each(0, 15, one)
        received[f] = sent[f]

    rsend[...] = operand(1)
    swap_f(rsend, rrecv, 4)
    lsend[...] = operand(0)
    swap_f(lsend, lrecv, 14)
    spread(wbsend.at[core], wbrecv.at[ch, core], 3)
    spread(hsend, hrecv.at[ch], 16)
    wbrecv[ch, core] = wbsend[core]
    hrecv[ch] = hsend[...]

    def regroup(received, grouped, where):
        for lc in range(2):
            work[where + lc, pl.ds(0, 256), :] = received[:, :, pl.ds(lc * 128, 128)].astype(F32).reshape(256, 128)
        for h in range(8):
            for kh in range(2):
                for lc in range(2):
                    grouped[h, :, pl.ds(kh * 256 + lc * 128, 128)] = work[
                        where + lc, pl.ds(kh * 8 + h, 16, stride=16), :].astype(BF16)

    wait_in(rrecv.at[pl.ds(0, 15)], 4)
    regroup(rrecv, rrows, 0)
    each(0, 7, lambda k: send(rrows.at[to_y(k)], rbuf.at[y, u], 11, dev_y(to_y(k))))
    rbuf[y, u] = rrows[y]
    wait_in(lrecv.at[pl.ds(0, 15)], 14)
    regroup(lrecv, lrows, 2)
    each(0, 7, lambda k: send(lrows.at[to_y(k)], lbuf.at[y, core], 6, dev_y(to_y(k))))
    lbuf[y, core] = lrows[y]

    wait_in(wbrecv.at[pl.ds(0, 7), 0], 3)
    send(wbrecv.at[:, core], wbrecv.at[:, core], 17, sibling)
    wait_in(wbrecv.at[:, 0], 17)
    gate = sigmoid(nn(wbrecv[:, 0].reshape(128, 128), zn)).T.reshape(8, 4, 2, 8, 128)
    for yy in range(8):
        for cc in range(2):
            gsend[yy * 2 + cc] = gate[yy, :, cc].reshape(32, 128).astype(BF16)

    def gate_b(k):
        y2, core2 = to_y(div(k, 2)), rem(core + 1 + k, 2)
        send(gsend.at[y2 * 2 + core2], g1.at[b], 5, ((y2 * 4 + z_lo) * 2 + core2, ch))

    each(0, 15, gate_b)
    g1[b] = gsend[b]

    wait_in(rbuf.at[pl.ds(0, 7), 0], 11)
    send(rbuf.at[:, u], rbuf.at[:, u], 15, place(x + 1 - 2 * u, z))
    wait_in(lbuf.at[pl.ds(0, 7), 0], 6)
    send(lbuf.at[:, core], lbuf.at[:, core], 12, sibling)

    wait_in(g1.at[pl.ds(0, 15)], 5)
    work[2, :, :] = g1[...].astype(F32).reshape(512, 128)
    for j in range(32):
        lo, high, parity, low = j % 16 // 4, j % 4 // 2, j // 16, j % 2
        g2send[j] = work[2, pl.ds(lo * 8 + high * 4 + parity * 2 + low, 16, stride=32), :].astype(BF16)

    def gate_e(k):
        x2, z2 = to_x(rem(k, 4)), to_z(div(k, 4))
        send(g2send.at[rem(x2, 2) * 16 + f_of(x2, z2)], g2.at[e], 7, place(x2, z2))

    each(0, 31, gate_e)
    g2[e] = g2send[e]

    wout_t = nt(eye.astype(BF16), wbrecv[:, 1].reshape(128, 128)).astype(BF16)
    wait_in(hrecv.at[pl.ds(0, 7)], 16)
    at_gain = iota((8, 16, 128), 1) == iota((8, 16, 128), 2)
    at_bias = iota((8, 16, 128), 1) + 16 == iota((8, 16, 128), 2)

    def column(where):
        col = jnp.sum(jnp.where(where, hrecv[...], 0.0), 2, keepdims=True)
        return jnp.broadcast_to(col, (8, 16, 128)).reshape(128, 128)

    hg, hb = column(at_gain), column(at_bias)
    lane = iota((256, 256), 0)
    natural = (bits(lane, 5, 2) * 64 + bits(lane, 2, 2) * 16 + bits(lane, 4, 1) * 8
               + bits(lane, 1, 1) * 4 + bits(lane, 7, 1) * 2 + bits(lane, 0, 1))
    perm = (natural == iota((256, 256), 1)).astype(BF16)

    wait_in(lbuf.at[:, 0], 12)
    wait_in(rbuf.at[:, 0], 15)
    tri = nt(rbuf[...].reshape(256, RES), lbuf[...].reshape(256, RES))
    tsend[...] = tri.astype(BF16).reshape(8, 2, 16, 256)

    for part in range(2):
        v = u + part * (1 - 2 * u)
        each(0, 7, lambda k: send(tsend.at[to_y(k), v], t1.at[part, y], 8 + part, dev_y(to_y(k))))
        t1[part, y] = tsend[y, v]

    wait_in(g2.at[pl.ds(0, 31)], 7)
    work[2, :, :] = g2[...].astype(F32).reshape(512, 128)
    gate_t = jnp.concatenate(
        [work[2, pl.ds(uu * 256 + bb, 16, stride=16), :] for uu in range(2) for bb in range(16)], axis=0).T

    for part in range(2):
        wait_in(t1.at[part, pl.ds(0, 7)], 8 + part)
        for lc in range(2):
            work[lc, pl.ds(0, 128), :] = t1[part, :, :, pl.ds(lc * 128, 128)].astype(F32).reshape(128, 128)
        for j in range(16):
            t2send[part * 16 + j] = jnp.concatenate(
                [work[lc, pl.ds(j, 8, stride=16), :] for lc in range(2)], axis=0).astype(BF16)

        def forward(k):
            x2, z2 = rem(x + (2 * rem(k + 1, 2) if part == 0 else 1 + 2 * rem(k, 2)), 4), to_z(div(k, 2))
            send(t2send.at[part * 16 + f_of(x2, z2)], t2.at[e], 10, place(x2, z2))

        each(0, 16 - (part == 0), forward)
    t2[e] = t2send[f]

    wait_in(t2.at[pl.ds(0, 31)], 10)
    tiles = t2[...].astype(F32).reshape(2, 16, 2, 8, 128)
    for lt in range(2):
        parts = []
        for uu in range(2):
            tri_ln = norm(tiles[uu, :, lt].reshape(128, 128), hg, hb).astype(BF16)
            at = uu * 256 + lt * 128
            parts.append((nn(wout_t, tri_ln) * gate_t[:, at:at + 128]).astype(BF16))
        update = nn(jnp.concatenate(parts, axis=1), perm)
        usend[:, :, pl.ds(lt * 256, 256)] = update.astype(BF16).reshape(8, 16, 256)

    def last(k):
        x2, half = to_x(div(k, 2)), rem(z_hi + k, 2)
        send(usend.at[x2 * 2 + half], out.at[e_ch], 18, place(x2, e_lo + 4 * half))

    each(0, 8, last)

    wait_out(zsend, 0)
    wait_out(warecv.at[pl.ds(0, 7), 0], 1)
    wait_out(warecv.at[:, 0], 2)
    wait_out(wbrecv.at[pl.ds(0, 7), 0], 3)
    wait_out(rsend.at[pl.ds(0, 15)], 4)
    wait_out(gsend.at[pl.ds(0, 15)], 5)
    wait_out(lrows.at[pl.ds(0, 7)], 6)
    wait_out(g2send.at[pl.ds(0, 31)], 7)
    wait_out(t1.at[0, pl.ds(0, 7)], 8)
    wait_out(t1.at[1, pl.ds(0, 7)], 9)
    wait_out(t2send.at[pl.ds(0, 31)], 10)
    wait_out(rrows.at[pl.ds(0, 7)], 11)
    wait_out(lbuf.at[:, 0], 12)
    wait_out(msend, 13)
    wait_out(lsend.at[pl.ds(0, 15)], 14)
    wait_out(rbuf.at[:, 0], 15)
    wait_out(hrecv.at[pl.ds(0, 7)], 16)
    wait_out(wbrecv.at[:, 0], 17)
    wait_out(usend, 18)
    wait_in(out, 18)


def body(pair, pair_mask, in_gain, in_bias, ab_weight, hid_gain, hid_bias, out_weight, gate_weight):
    rows = pair.shape[1]
    scratch = [
        ((16, rows, RES), BF16), ((rows, RES), jnp.int32), ((2, 32, 128), BF16),
        ((1, CH), F32), ((1, CH), F32), ((2, 16, 128), BF16), ((1, 16), F32), ((1, 16), F32),
        ((4, 512, 128), F32),
        ((8, 16, RES), BF16), ((8, 16, RES), BF16),
        ((8, 2, 32, 128), BF16), ((8, 2, 16, 128), BF16),
        ((1, 128), F32), ((8, 1, 128), F32),
        ((8, 128), F32), ((8, 128), F32),
        ((16, 16, 256), BF16), ((16, 16, 256), BF16), ((16, 16, 256), BF16), ((16, 16, 256), BF16),
        ((8, 16, RES), BF16), ((8, 16, RES), BF16), ((8, 2, 16, RES), BF16), ((8, 2, 16, RES), BF16),
        ((8, 2, 16, 256), BF16), ((2, 8, 16, 256), BF16),
        ((32, 16, 128), BF16), ((32, 16, 128), BF16),
        ((16, 32, 128), BF16), ((16, 32, 128), BF16),
        ((32, 16, 128), BF16), ((32, 16, 128), BF16),
        ((8, 16, RES), BF16),
    ]
    swapped = pl.pallas_call(
        kernel,
        out_shape=jax.ShapeDtypeStruct((8, 16, RES), BF16),
        in_specs=[pl.BlockSpec(memory_space=pltpu.HBM)] * 9,
        out_specs=pl.BlockSpec(memory_space=pltpu.VMEM),
        scratch_shapes=[pltpu.VMEM(shape, kind) for shape, kind in scratch]
        + [pltpu.SemaphoreType.DMA((9,)), pltpu.SemaphoreType.DMA((19,)), pltpu.SemaphoreType.DMA((19,))],
        compiler_params=pltpu.CompilerParams(
            collective_id=0, has_side_effects=True, vmem_limit_bytes=VMEM_LIMIT),
    )(pair, pair_mask, jnp.swapaxes(ab_weight, 1, 2).reshape(2, 32, CH), in_gain.reshape(1, CH), in_bias.reshape(1, CH),
      gate_weight.T, out_weight, hid_gain.reshape(1, 16), hid_bias.reshape(1, 16))
    return jnp.swapaxes(swapped, 0, 1)


def solution(mesh):
    placed = (
        P("ch", "dap", None),
        P("dap", None),
        P(),
        P(),
        P(None, None, "ch"),
        P("ch"),
        P("ch"),
        P("ch", None),
        P(None, "ch"),
    )
    return jax.shard_map(
        body, mesh=mesh, in_specs=placed, out_specs=P("ch", "dap", None), check_vma=False
    )
```

time: 68.5 us -> 63.1 us (0.921)
  the two profiles are of different devices: /device:TPU:1 before, /device:TPU:8 now
where the time goes in v3:
time: 63.1 us; the launch traced here: 62.9 us
  Pallas kernels  61.3 us (97%)
  local copies, waits for them, and re-layouts  1.64 us (3%)
    pallas_call x1, Pallas kernels, body(): pl.pallas_call(kernel, out_shape=jax.ShapeDtypeStruct((8, 16, RES), BF16)...  61.3 us
    transpose x1, local copies, waits for them, and re-layouts, body(): return jnp.swapaxes(swapped, 0, 1)  1.64 us

profile of v3, /device:TPU:8, one launch (start us, length us, event | category | flops | bytes accessed | tf_op | source)
XLA Modules:
  0.0 62.9 jit_solution(7191420880052360043)
XLA Ops:
  0.0 61.3 %shard_map.91 = bf16[8,16,512]{2,1,0:T(8,128)(2,1)} custom-call(bf16[16,8,512]{2,1,0:T(8,128)(2,1)} %pair_in.1, s32[8,512]{1,0:T(8,128)} %mask_in.1, bf16[2,32,128]{2,1,0:T(8,128)(2,1)} %bitcast.10, f32[1,128]{1,0:T(1,128)} %bitcast.12, f32[1,128]{1,0:T(1,128)} %bitcast.13, bf16[16,128]{1,0:T(8,128)(2,1)} %bitcast.11, bf16[16,128]{1,0:T(8,128)(2,1)} %out_in.1, ...), custom_call_target="tpu_custom_call" | custom-call | tf_op jit(solution)/shard_map/pallas_call | solution.py:344
  61.3 1.6 %copy.10 = bf16[16,8,512]{2,1,0:T(8,128)(2,1)} copy(bf16[16,8,512]{2,0,1:T(8,128)(2,1)} %bitcast.9) | data formatting | bytes 262144 | tf_op jit(solution)/shard_map/transpose | solution.py:355

commit v4 on v3

v4 whole, which is shorter than its diff:
```python
import jax
import jax.numpy as jnp
from jax import lax
from jax.experimental import pallas as pl
from jax.experimental.pallas import tpu as pltpu
from jax.sharding import PartitionSpec as P

CH = 128
RES = 512
EPS = 1e-05
VMEM_LIMIT = 62 * 1024 * 1024
MESH = pl.DeviceIdType.MESH
F32 = jnp.float32
BF16 = jnp.bfloat16


def nt(a, b):
    return lax.dot_general(a, b, (((1,), (1,)), ((), ())), preferred_element_type=F32)


def nn(a, b):
    return lax.dot_general(a, b, (((1,), (0,)), ((), ())), preferred_element_type=F32)


def iota(shape, dim):
    return lax.broadcasted_iota(jnp.int32, shape, dim)


def bits(value, low, count):
    return lax.shift_right_logical(value, low) & ((1 << count) - 1)


def sigmoid(x):
    return 1.0 / (1.0 + jnp.exp(-x))


def norm(values, gain, bias):
    mean = jnp.sum(values, 0, keepdims=True) * (1.0 / CH)
    square = jnp.sum(values * values, 0, keepdims=True) * (1.0 / CH)
    var = square - mean * mean
    return (values - mean) * lax.rsqrt(var + EPS) * gain + bias


def each(first, last, body):
    def step(k, carry):
        body(k)
        return carry
    lax.fori_loop(first, last, step, 0, unroll=True)


def far(n, top):
    return top + lax.div(n + 1, 2) * (1 - 2 * lax.rem(n, 2))


def kernel(pair_in, mask_in, ab_in, gain_in, bias_in, gate_in, out_in, hid_gain_in, hid_bias_in, out,
           pair, mask, wsend, gain, bias, hid_gain, hid_bias,
           work, zsend, zrecv, wrecv, hsend, hrecv, msend, mrecv,
           rsend, rrecv, rrows, rbuf, lsend, lmid, lrows, lrecv, lbuf, tsend, t1, t2send, t2, gsend, g1, g2send, g2, usend,
           lsem, ssem, rsem):
    div, rem = lax.div, lax.rem
    dap = lax.axis_index("dap")
    ch = lax.axis_index("ch")
    x, z_hi = div(ch, 2), rem(ch, 2)
    y, z_lo, core = div(dap, 8), rem(div(dap, 2), 4), rem(dap, 2)
    z = z_hi * 4 + z_lo
    b = y * 2 + core
    e_lo, s = rem(z + 2, 4), div(rem(z + 6, 8), 4)
    e_ch = 2 * x + s
    u = rem(x, 2)
    f = e_lo * 4 + div(x, 2) * 2 + s
    e = u * 16 + f

    def place(x2, z2):
        return ((y * 4 + rem(z2, 4)) * 2 + core, x2 * 2 + div(z2, 4))

    def f_of(x2, z2):
        return rem(z2 + 2, 4) * 4 + div(x2, 2) * 2 + div(rem(z2 + 6, 8), 4)

    def dev_y(y2):
        return ((y2 * 4 + z_lo) * 2 + core, ch)

    sibling = (dap + 1 - 2 * core, ch)

    def send(src, dst, sem, device):
        pltpu.make_async_remote_copy(
            src_ref=src, dst_ref=dst, send_sem=ssem.at[sem], recv_sem=rsem.at[sem],
            device_id=device, device_id_type=MESH).start()

    def wait_in(ref, sem):
        pltpu.make_async_copy(ref, ref, rsem.at[sem]).wait()

    def wait_out(ref, sem):
        pltpu.make_async_copy(ref, ref, ssem.at[sem]).wait()

    def to_x(k):
        return rem(x + far(k, 2), 4)

    def to_y(k):
        return rem(y + far(k, 4), 8)

    def to_z(k):
        return rem(z + far(k, 4), 8)

    loads = [
        pltpu.make_async_copy(source, target, lsem.at[i]) for i, (source, target) in enumerate((
            (pair_in, pair), (mask_in, mask), (ab_in, wsend.at[:, pl.ds(0, 32)]),
            (gate_in, wsend.at[0, pl.ds(32, 16)]), (out_in, wsend.at[1, pl.ds(32, 16)]),
            (gain_in, gain), (bias_in, bias), (hid_gain_in, hid_gain), (hid_bias_in, hid_bias)))
    ]
    for load in loads:
        load.start()

    barrier = pltpu.get_barrier_semaphore()

    def greet(device):
        pl.semaphore_signal(barrier, inc=1, device_id=device, device_id_type=MESH)

    def greet_y(k):
        y2 = to_y(div(k, 2))
        greet(((y2 * 4 + z_lo) * 2 + rem(core + 1 + k, 2), ch))

    each(0, 15, greet_y)
    each(0, 19, lambda k: greet(place(to_x(div(k, 5)), to_z(rem(k, 5) + 3))))

    for load in loads:
        load.wait()
    for kc in range(4):
        work[kc, pl.ds(0, 128), :] = pair[:, :, pl.ds(kc * 128, 128)].astype(F32).reshape(128, 128)
    for kc in range(4):
        for r in range(8):
            zsend[r, :, pl.ds(kc * 128, 128)] = work[kc, pl.ds(r, 16, stride=8), :].astype(BF16)
    own_mask = mask[pl.ds(ch, 1), :].astype(F32)
    for kc in range(4):
        msend[pl.ds(kc, 1), :] = own_mask[:, kc * 128:kc * 128 + 128]

    pl.semaphore_wait(barrier, 34)

    def first(k):
        x2, s2 = to_x(div(k, 2)), rem(s + k, 2)
        send(zsend.at[x2 * 2 + s2], zrecv.at[ch], 0, place(x2, rem(z_lo + 2 + 4 * s2, 8)))

    z6 = 4 * (1 - z_hi) + 2 * (1 - div(z_lo, 2)) + rem(z_lo, 2)
    crossed = x * 2 + 1 - z_hi

    def along_x(src, dst, sem):
        each(0, 3, lambda k: send(src, dst, sem, place(to_x(k), z)))

    send(wsend.at[core], wrecv.at[ch, core], 1, place(x, z6))
    each(0, 8, first)
    send(msend, mrecv, 13, place(x, rem(z_lo + 2 + 4 * z_hi, 8)))
    along_x(wsend.at[core], wrecv.at[ch, core], 2)
    wrecv[ch, core] = wsend[core]

    eye = iota((128, 128), 0) == iota((128, 128), 1)
    gain_col = jnp.sum(jnp.where(eye, gain[...], 0.0), 1, keepdims=True)
    bias_col = jnp.sum(jnp.where(eye, bias[...], 0.0), 1, keepdims=True)
    hsend[...] = jnp.zeros((1, 128), F32)
    hsend[:, pl.ds(0, 16)] = hid_gain[...]
    hsend[:, pl.ds(16, 16)] = hid_bias[...]

    wait_in(wrecv.at[0, 0], 1)
    along_x(wrecv.at[crossed, core], wrecv.at[crossed, core], 3)
    wait_in(zrecv, 0)
    wait_in(wrecv.at[pl.ds(0, 3), 0], 2)
    wait_in(wrecv.at[pl.ds(0, 3), 0], 3)
    send(wrecv.at[:, core], wrecv.at[:, core], 17, sibling)
    zn = norm(zrecv[...].astype(F32).reshape(128, RES), gain_col, bias_col).astype(BF16)
    wait_in(mrecv, 13)
    masking = jnp.concatenate([mrecv[pl.ds(kc, 1), :] for kc in range(4)], axis=1)
    wait_in(wrecv.at[:, 0], 17)

    def operand(side):
        opened = sigmoid(nn(wrecv[:, side, pl.ds(0, 16)].reshape(128, 128), zn))
        value = nn(wrecv[:, side, pl.ds(16, 16)].reshape(128, 128), zn)
        return opened * value * masking

    def swap_f(sent, received, sem):
        def one(k):
            x2, z2 = rem(x + 2 * rem(k + 1, 2), 4), to_z(div(k, 2))
            send(sent.at[f_of(x2, z2)], received.at[f], sem, place(x2, z2))
        each(0, 15, one)
        received[f] = sent[f]

    def swap_y(sent, slot, sem):
        each(0, 7, lambda k: send(sent.at[to_y(k)], slot, sem, dev_y(to_y(k))))

    right = operand(1).reshape(16, 8, RES)
    for kh in range(2):
        at = kh * 256
        rsend[kh] = jnp.concatenate([right[:, :, at:at + 128], right[:, :, at + 128:at + 256]], axis=1).astype(BF16)
        swap_f(rsend.at[kh], rrecv.at[kh], 4 + 15 * kh)
    left = operand(0)
    for lc in range(4):
        work[lc, pl.ds(0, 128), :] = left[:, lc * 128:lc * 128 + 128]
    for lc in range(4):
        for h in range(8):
            lsend[h, :, pl.ds(lc * 128, 128)] = work[lc, pl.ds(h, 16, stride=8), :].astype(BF16)
    swap_y(lsend, lmid.at[y], 14)
    lmid[y] = lsend[y]
    each(0, 4, lambda k: send(hsend, hrecv.at[ch], 16, place(to_x(k), z6)))
    along_x(hsend, hrecv.at[ch], 16)
    hrecv[ch] = hsend[...]

    gate = sigmoid(nn(wrecv[:, 0, pl.ds(32, 16)].reshape(128, 128), zn)).T.reshape(8, 4, 2, 8, 128)
    for yy in range(8):
        for cc in range(2):
            gsend[yy * 2 + cc] = gate[yy, :, cc].reshape(32, 128).astype(BF16)

    def gate_b(k):
        y2, core2 = to_y(div(k, 2)), rem(core + 1 + k, 2)
        send(gsend.at[y2 * 2 + core2], g1.at[b], 5, ((y2 * 4 + z_lo) * 2 + core2, ch))

    each(0, 15, gate_b)
    g1[b] = gsend[b]

    def spread_right(kh):
        wait_in(rrecv.at[kh, pl.ds(0, 15)], 4 + 15 * kh)
        work[kh, pl.ds(0, 256), :] = rrecv[kh].astype(F32).reshape(256, 128)
        for h in range(8):
            for lc in range(2):
                rrows[kh, h, :, pl.ds(lc * 128, 128)] = work[kh, pl.ds(lc * 8 + h, 16, stride=16), :].astype(BF16)
        swap_y(rrows.at[kh], rbuf.at[kh, y, u], 11 + 9 * kh)
        rbuf[kh, y, u] = rrows[kh, y]

    spread_right(0)
    wait_in(lmid.at[pl.ds(0, 7)], 14)
    for lc in range(4):
        work[lc, pl.ds(256, 128), :] = lmid[:, :, pl.ds(lc * 128, 128)].astype(F32).reshape(128, 128)
    for g in range(16):
        for lc in range(2):
            lrows[g, :, pl.ds(lc * 128, 128)] = jnp.concatenate(
                [work[kh * 2 + lc, pl.ds(256 + g, 8, stride=16), :] for kh in range(2)], axis=0).astype(BF16)
    swap_f(lrows, lrecv, 6)
    spread_right(1)

    for kh in range(2):
        wait_in(rbuf.at[0, pl.ds(0, 7), 0], 11 + 9 * kh)
        send(rbuf.at[kh, :, u], rbuf.at[kh, :, u], 15 + 6 * kh, place(x + 1 - 2 * u, z))

    wout_t = nt(eye.astype(BF16), wrecv[:, 1, pl.ds(32, 16)].reshape(128, 128)).astype(BF16)
    wait_in(hrecv.at[pl.ds(0, 7)], 16)
    at_gain = iota((8, 16, 128), 1) == iota((8, 16, 128), 2)
    at_bias = iota((8, 16, 128), 1) + 16 == iota((8, 16, 128), 2)

    def column(where):
        col = jnp.sum(jnp.where(where, hrecv[...], 0.0), 2, keepdims=True)
        return jnp.broadcast_to(col, (8, 16, 128)).reshape(128, 128)

    hg, hb = column(at_gain), column(at_bias)
    lane = iota((256, 256), 0)
    natural = (bits(lane, 5, 2) * 64 + bits(lane, 2, 2) * 16 + bits(lane, 4, 1) * 8
               + bits(lane, 1, 1) * 4 + bits(lane, 7, 1) * 2 + bits(lane, 0, 1))
    perm = (natural == iota((256, 256), 1)).astype(BF16)

    wait_in(lrecv.at[pl.ds(0, 15)], 6)
    for lc in range(2):
        work[2 + lc, pl.ds(0, 256), :] = lrecv[:, :, pl.ds(lc * 128, 128)].astype(F32).reshape(256, 128)
    for kh in range(2):
        for yy in range(8):
            for lc in range(2):
                lbuf[kh, yy, core, :, pl.ds(lc * 128, 128)] = work[2 + lc, pl.ds(kh * 8 + yy, 16, stride=16), :].astype(BF16)
    send(lbuf.at[:, :, core], lbuf.at[:, :, core], 12, sibling)
    wait_in(rbuf.at[0, :, 0], 15)
    wait_in(rbuf.at[1, :, 0], 21)
    wait_in(lbuf.at[:, :, 0], 12)
    tri = nt(rbuf[0].reshape(256, 256), lbuf[0].reshape(256, 256)) + nt(rbuf[1].reshape(256, 256), lbuf[1].reshape(256, 256))
    tsend[...] = tri.astype(BF16).reshape(8, 2, 16, 256)

    for v in range(2):
        each(0, 7, lambda k: send(tsend.at[to_y(k), v], t1.at[v, y], 8 + v, dev_y(to_y(k))))
        t1[v, y] = tsend[y, v]

    wait_in(g1.at[pl.ds(0, 15)], 5)
    work[2, :, :] = g1[...].astype(F32).reshape(512, 128)
    for j in range(32):
        lo, high, parity, low = j % 16 // 4, j % 4 // 2, j // 16, j % 2
        g2send[j] = work[2, pl.ds(lo * 8 + high * 4 + parity * 2 + low, 16, stride=32), :].astype(BF16)

    def gate_e(k):
        x2, z2 = to_x(rem(k, 4)), to_z(div(k, 4))
        send(g2send.at[rem(x2, 2) * 16 + f_of(x2, z2)], g2.at[e], 7, place(x2, z2))

    each(0, 31, gate_e)
    g2[e] = g2send[e]

    for v in range(2):
        wait_in(t1.at[v, pl.ds(0, 7)], 8 + v)
        for lc in range(2):
            work[lc, pl.ds(0, 128), :] = t1[v, :, :, pl.ds(lc * 128, 128)].astype(F32).reshape(128, 128)
        for j in range(16):
            t2send[v * 16 + j] = jnp.concatenate(
                [work[lc, pl.ds(j, 8, stride=16), :] for lc in range(2)], axis=0).astype(BF16)
        w = rem(u + v, 2)

        def forward(k):
            x2, z2 = rem(x + 2 - w + rem(k, 2) * (4 * w - 2), 4), to_z(div(k, 2))
            send(t2send.at[v * 16 + f_of(x2, z2)], t2.at[e], 10, place(x2, z2))

        each(0, 15, forward)

        @pl.when(w == 1)
        def _():
            forward(15)

        @pl.when(w == 0)
        def _():
            t2[e] = t2send[v * 16 + f]

    wait_in(g2.at[pl.ds(0, 31)], 7)
    work[2, :, :] = g2[...].astype(F32).reshape(512, 128)
    gate_t = jnp.concatenate(
        [work[2, pl.ds(uu * 256 + bb, 16, stride=16), :] for uu in range(2) for bb in range(16)], axis=0).T

    wait_in(t2.at[pl.ds(0, 31)], 10)
    tiles = t2[...].astype(F32).reshape(2, 16, 2, 8, 128)
    for lt in range(2):
        parts = []
        for uu in range(2):
            tri_ln = norm(tiles[uu, :, lt].reshape(128, 128), hg, hb).astype(BF16)
            at = uu * 256 + lt * 128
            parts.append((nn(wout_t, tri_ln) * gate_t[:, at:at + 128]).astype(BF16))
        update = nn(jnp.concatenate(parts, axis=1), perm)
        usend[lt] = update.astype(BF16).reshape(8, 16, 256)

        def last(k):
            x2, half = to_x(div(k, 2)), rem(z_hi + k, 2)
            send(usend.at[lt, x2 * 2 + half], out.at[e_ch, :, pl.ds(lt * 256, 256)], 18, place(x2, e_lo + 4 * half))

        each(0, 8, last)

    wait_out(zsend, 0)
    wait_out(wsend.at[0], 1)
    wait_out(wrecv.at[pl.ds(0, 3), 0], 2)
    wait_out(wrecv.at[pl.ds(0, 3), 0], 3)
    wait_out(rsend.at[0, pl.ds(0, 15)], 4)
    wait_out(rsend.at[1, pl.ds(0, 15)], 19)
    wait_out(lsend.at[pl.ds(0, 7)], 14)
    wait_out(gsend.at[pl.ds(0, 15)], 5)
    wait_out(lrows.at[pl.ds(0, 15)], 6)
    wait_out(g2send.at[pl.ds(0, 31)], 7)
    wait_out(t1.at[0, pl.ds(0, 7)], 8)
    wait_out(t1.at[1, pl.ds(0, 7)], 9)
    wait_out(t2send.at[pl.ds(0, 31)], 10)
    wait_out(rrows.at[0, pl.ds(0, 7)], 11)
    wait_out(rrows.at[1, pl.ds(0, 7)], 20)
    wait_out(lbuf.at[:, :, 0], 12)
    wait_out(msend, 13)
    wait_out(rbuf.at[0, :, 0], 15)
    wait_out(rbuf.at[1, :, 0], 21)
    wait_out(hrecv.at[pl.ds(0, 7)], 16)
    wait_out(wrecv.at[:, 0], 17)
    wait_out(usend, 18)
    wait_in(out, 18)


def body(pair, pair_mask, in_gain, in_bias, ab_weight, hid_gain, hid_bias, out_weight, gate_weight):
    rows = pair.shape[1]
    scratch = [
        ((16, rows, RES), BF16), ((rows, RES), jnp.int32), ((2, 48, 128), BF16),
        ((1, CH), F32), ((1, CH), F32), ((1, 16), F32), ((1, 16), F32),
        ((4, 512, 128), F32),
        ((8, 16, RES), BF16), ((8, 16, RES), BF16),
        ((8, 2, 48, 128), BF16),
        ((1, 128), F32), ((8, 1, 128), F32),
        ((8, 128), F32), ((8, 128), F32),
        ((2, 16, 16, 128), BF16), ((2, 16, 16, 128), BF16), ((2, 8, 16, 256), BF16), ((2, 8, 2, 16, 256), BF16),
        ((8, 16, RES), BF16), ((8, 16, RES), BF16), ((16, 16, 256), BF16), ((16, 16, 256), BF16), ((2, 8, 2, 16, 256), BF16),
        ((8, 2, 16, 256), BF16), ((2, 8, 16, 256), BF16),
        ((32, 16, 128), BF16), ((32, 16, 128), BF16),
        ((16, 32, 128), BF16), ((16, 32, 128), BF16),
        ((32, 16, 128), BF16), ((32, 16, 128), BF16),
        ((2, 8, 16, 256), BF16),
    ]
    swapped = pl.pallas_call(
        kernel,
        out_shape=jax.ShapeDtypeStruct((8, 16, RES), BF16),
        in_specs=[pl.BlockSpec(memory_space=pltpu.HBM)] * 9,
        out_specs=pl.BlockSpec(memory_space=pltpu.VMEM),
        scratch_shapes=[pltpu.VMEM(shape, kind) for shape, kind in scratch]
        + [pltpu.SemaphoreType.DMA((9,)), pltpu.SemaphoreType.DMA((22,)), pltpu.SemaphoreType.DMA((22,))],
        compiler_params=pltpu.CompilerParams(
            collective_id=0, has_side_effects=True, vmem_limit_bytes=VMEM_LIMIT),
    )(pair, pair_mask, jnp.swapaxes(ab_weight, 1, 2).reshape(2, 32, CH), in_gain.reshape(1, CH), in_bias.reshape(1, CH),
      gate_weight.T, out_weight, hid_gain.reshape(1, 16), hid_bias.reshape(1, 16))
    return jnp.swapaxes(swapped, 0, 1)


def solution(mesh):
    placed = (
        P("ch", "dap", None),
        P("dap", None),
        P(),
        P(),
        P(None, None, "ch"),
        P("ch"),
        P("ch"),
        P("ch", None),
        P(None, "ch"),
    )
    return jax.shard_map(
        body, mesh=mesh, in_specs=placed, out_specs=P("ch", "dap", None), check_vma=False
    )
```

time: 63.1 us -> 59 us (0.935)
  the two profiles are of different devices: /device:TPU:8 before, /device:TPU:1 now
where the time goes in v4:
time: 59 us; the launch traced here: 58.9 us
  Pallas kernels  57.2 us (97%)
  local copies, waits for them, and re-layouts  1.64 us (3%)
    pallas_call x1, Pallas kernels, body(): pl.pallas_call(kernel, out_shape=jax.ShapeDtypeStruct((8, 16, RES), BF16)...  57.2 us
    transpose x1, local copies, waits for them, and re-layouts, body(): return jnp.swapaxes(swapped, 0, 1)  1.64 us

profile of v4, /device:TPU:1, one launch (start us, length us, event | category | flops | bytes accessed | tf_op | source)
XLA Modules:
  0.0 58.9 jit_solution(3761233814709820751)
XLA Ops:
  0.0 57.2 %shard_map.91 = bf16[8,16,512]{2,1,0:T(8,128)(2,1)} custom-call(bf16[16,8,512]{2,1,0:T(8,128)(2,1)} %pair_in.1, s32[8,512]{1,0:T(8,128)} %mask_in.1, bf16[2,32,128]{2,1,0:T(8,128)(2,1)} %bitcast.10, f32[1,128]{1,0:T(1,128)} %bitcast.12, f32[1,128]{1,0:T(1,128)} %bitcast.13, bf16[16,128]{1,0:T(8,128)(2,1)} %bitcast.11, bf16[16,128]{1,0:T(8,128)(2,1)} %out_in.1, ...), custom_call_target="tpu_custom_call" | custom-call | tf_op jit(solution)/shard_map/pallas_call | solution.py:374
  57.3 1.6 %copy.10 = bf16[16,8,512]{2,1,0:T(8,128)(2,1)} copy(bf16[16,8,512]{2,0,1:T(8,128)(2,1)} %bitcast.9) | data formatting | bytes 262144 | tf_op jit(solution)/shard_map/transpose | solution.py:385

commit v5 on v4

--- a/solution.py
+++ b/solution.py
@@ -115,12 +115,12 @@
     def greet(device):
         pl.semaphore_signal(barrier, inc=1, device_id=device, device_id_type=MESH)
 
-    def greet_y(k):
-        y2 = to_y(div(k, 2))
-        greet(((y2 * 4 + z_lo) * 2 + rem(core + 1 + k, 2), ch))
-
-    each(0, 15, greet_y)
-    each(0, 19, lambda k: greet(place(to_x(div(k, 5)), to_z(rem(k, 5) + 3))))
+    greet(dev_y(rem(y + 4, 8)))
+    each(0, 8, lambda k: greet(place(to_x(div(k, 2)), rem(z + 2 + 4 * rem(k, 2), 8))))
+    each(1, 7, lambda k: greet(dev_y(to_y(k))))
+    each(0, 3, lambda k: greet(place(to_x(k), z)))
+    each(0, 2, lambda k: greet(place(x, rem(z + 1 + 6 * k, 8))))
+    greet(sibling)
 
     for load in loads:
         load.wait()
@@ -133,7 +133,7 @@
     for kc in range(4):
         msend[pl.ds(kc, 1), :] = own_mask[:, kc * 128:kc * 128 + 128]
 
-    pl.semaphore_wait(barrier, 34)
+    pl.semaphore_wait(barrier, 21)
 
     def first(k):
         x2, s2 = to_x(div(k, 2)), rem(s + k, 2)
@@ -145,10 +145,12 @@
     def along_x(src, dst, sem):
         each(0, 3, lambda k: send(src, dst, sem, place(to_x(k), z)))
 
-    send(wsend.at[core], wrecv.at[ch, core], 1, place(x, z6))
+    each(0, 4, lambda k: send(wsend.at[core, pl.ds(0, 32)], wrecv.at[ch, core, pl.ds(0, 32)], 2, place(to_x(k), z6)))
+    along_x(wsend.at[core, pl.ds(0, 32)], wrecv.at[ch, core, pl.ds(0, 32)], 2)
     each(0, 8, first)
+    each(0, 4, lambda k: send(wsend.at[core, pl.ds(32, 16)], wrecv.at[ch, core, pl.ds(32, 16)], 3, place(to_x(k), z6)))
+    along_x(wsend.at[core, pl.ds(32, 16)], wrecv.at[ch, core, pl.ds(32, 16)], 3)
     send(msend, mrecv, 13, place(x, rem(z_lo + 2 + 4 * z_hi, 8)))
-    along_x(wsend.at[core], wrecv.at[ch, core], 2)
     wrecv[ch, core] = wsend[core]
 
     eye = iota((128, 128), 0) == iota((128, 128), 1)
@@ -158,16 +160,13 @@
     hsend[:, pl.ds(0, 16)] = hid_gain[...]
     hsend[:, pl.ds(16, 16)] = hid_bias[...]
 
-    wait_in(wrecv.at[0, 0], 1)
-    along_x(wrecv.at[crossed, core], wrecv.at[crossed, core], 3)
+    wait_in(wrecv.at[pl.ds(0, 7), 0, pl.ds(0, 32)], 2)
+    send(wrecv.at[:, core, pl.ds(0, 32)], wrecv.at[:, core, pl.ds(0, 32)], 17, sibling)
     wait_in(zrecv, 0)
-    wait_in(wrecv.at[pl.ds(0, 3), 0], 2)
-    wait_in(wrecv.at[pl.ds(0, 3), 0], 3)
-    send(wrecv.at[:, core], wrecv.at[:, core], 17, sibling)
     zn = norm(zrecv[...].astype(F32).reshape(128, RES), gain_col, bias_col).astype(BF16)
     wait_in(mrecv, 13)
     masking = jnp.concatenate([mrecv[pl.ds(kc, 1), :] for kc in range(4)], axis=1)
-    wait_in(wrecv.at[:, 0], 17)
+    wait_in(wrecv.at[:, 0, pl.ds(0, 32)], 17)
 
     def operand(side):
         opened = sigmoid(nn(wrecv[:, side, pl.ds(0, 16)].reshape(128, 128), zn))
@@ -201,6 +200,9 @@
     along_x(hsend, hrecv.at[ch], 16)
     hrecv[ch] = hsend[...]
 
+    wait_in(wrecv.at[pl.ds(0, 7), 0, pl.ds(32, 16)], 3)
+    send(wrecv.at[:, core, pl.ds(32, 16)], wrecv.at[:, core, pl.ds(32, 16)], 1, sibling)
+    wait_in(wrecv.at[:, 0, pl.ds(32, 16)], 1)
     gate = sigmoid(nn(wrecv[:, 0, pl.ds(32, 16)].reshape(128, 128), zn)).T.reshape(8, 4, 2, 8, 128)
     for yy in range(8):
         for cc in range(2):
@@ -329,9 +331,9 @@
         each(0, 8, last)
 
     wait_out(zsend, 0)
-    wait_out(wsend.at[0], 1)
-    wait_out(wrecv.at[pl.ds(0, 3), 0], 2)
-    wait_out(wrecv.at[pl.ds(0, 3), 0], 3)
+    wait_out(wrecv.at[:, 0, pl.ds(32, 16)], 1)
+    wait_out(wrecv.at[pl.ds(0, 7), 0, pl.ds(0, 32)], 2)
+    wait_out(wrecv.at[pl.ds(0, 7), 0, pl.ds(32, 16)], 3)
     wait_out(rsend.at[0, pl.ds(0, 15)], 4)
     wait_out(rsend.at[1, pl.ds(0, 15)], 19)
     wait_out(lsend.at[pl.ds(0, 7)], 14)
@@ -348,7 +350,7 @@
     wait_out(rbuf.at[0, :, 0], 15)
     wait_out(rbuf.at[1, :, 0], 21)
     wait_out(hrecv.at[pl.ds(0, 7)], 16)
-    wait_out(wrecv.at[:, 0], 17)
+    wait_out(wrecv.at[:, 0, pl.ds(0, 32)], 17)
     wait_out(usend, 18)
     wait_in(out, 18)
 

time: 59 us -> 57.7 us (0.978)
  the two profiles are of different devices: /device:TPU:1 before, /device:TPU:2 now
where the time goes in v5:
time: 57.7 us; the launch traced here: 57.5 us
  Pallas kernels  55.9 us (97%)
  local copies, waits for them, and re-layouts  1.64 us (3%)
    pallas_call x1, Pallas kernels, body(): pl.pallas_call(kernel, out_shape=jax.ShapeDtypeStruct((8, 16, RES), BF16)...  55.9 us
    transpose x1, local copies, waits for them, and re-layouts, body(): return jnp.swapaxes(swapped, 0, 1)  1.64 us

profile of v5, /device:TPU:2, one launch (start us, length us, event | category | flops | bytes accessed | tf_op | source)
XLA Modules:
  0.0 57.5 jit_solution(8769354551162406519)
XLA Ops:
  0.0 55.9 %shard_map.91 = bf16[8,16,512]{2,1,0:T(8,128)(2,1)} custom-call(bf16[16,8,512]{2,1,0:T(8,128)(2,1)} %pair_in.1, s32[8,512]{1,0:T(8,128)} %mask_in.1, bf16[2,32,128]{2,1,0:T(8,128)(2,1)} %bitcast.10, f32[1,128]{1,0:T(1,128)} %bitcast.12, f32[1,128]{1,0:T(1,128)} %bitcast.13, bf16[16,128]{1,0:T(8,128)(2,1)} %bitcast.11, bf16[16,128]{1,0:T(8,128)(2,1)} %out_in.1, ...), custom_call_target="tpu_custom_call" | custom-call | tf_op jit(solution)/shard_map/pallas_call | solution.py:376
  55.9 1.6 %copy.10 = bf16[16,8,512]{2,1,0:T(8,128)(2,1)} copy(bf16[16,8,512]{2,0,1:T(8,128)(2,1)} %bitcast.9) | data formatting | bytes 262144 | tf_op jit(solution)/shard_map/transpose | solution.py:387

commit v6 on v5

--- a/solution.py
+++ b/solution.py
@@ -184,10 +184,13 @@
         each(0, 7, lambda k: send(sent.at[to_y(k)], slot, sem, dev_y(to_y(k))))
 
     right = operand(1).reshape(16, 8, RES)
-    for kh in range(2):
+
+    def swap_right(kh):
         at = kh * 256
         rsend[kh] = jnp.concatenate([right[:, :, at:at + 128], right[:, :, at + 128:at + 256]], axis=1).astype(BF16)
         swap_f(rsend.at[kh], rrecv.at[kh], 4 + 15 * kh)
+
+    swap_right(0)
     left = operand(0)
     for lc in range(4):
         work[lc, pl.ds(0, 128), :] = left[:, lc * 128:lc * 128 + 128]
@@ -196,8 +199,7 @@
             lsend[h, :, pl.ds(lc * 128, 128)] = work[lc, pl.ds(h, 16, stride=8), :].astype(BF16)
     swap_y(lsend, lmid.at[y], 14)
     lmid[y] = lsend[y]
-    each(0, 4, lambda k: send(hsend, hrecv.at[ch], 16, place(to_x(k), z6)))
-    along_x(hsend, hrecv.at[ch], 16)
+    swap_right(1)
     hrecv[ch] = hsend[...]
 
     wait_in(wrecv.at[pl.ds(0, 7), 0, pl.ds(32, 16)], 3)
@@ -215,12 +217,17 @@
     each(0, 15, gate_b)
     g1[b] = gsend[b]
 
+    each(0, 4, lambda k: send(hsend, hrecv.at[ch], 16, place(to_x(k), z6)))
+    along_x(hsend, hrecv.at[ch], 16)
+
     def spread_right(kh):
         wait_in(rrecv.at[kh, pl.ds(0, 15)], 4 + 15 * kh)
         work[kh, pl.ds(0, 256), :] = rrecv[kh].astype(F32).reshape(256, 128)
         for h in range(8):
             for lc in range(2):
                 rrows[kh, h, :, pl.ds(lc * 128, 128)] = work[kh, pl.ds(lc * 8 + h, 16, stride=16), :].astype(BF16)
+        if kh == 1:
+            each(0, 8, lambda k: send(rrows.at[1, to_y(k)], rbuf.at[1, y, u], 20, (dev_y(to_y(k))[0], ch + 2 - 4 * u)))
         swap_y(rrows.at[kh], rbuf.at[kh, y, u], 11 + 9 * kh)
         rbuf[kh, y, u] = rrows[kh, y]
 
@@ -235,9 +242,8 @@
     swap_f(lrows, lrecv, 6)
     spread_right(1)
 
-    for kh in range(2):
-        wait_in(rbuf.at[0, pl.ds(0, 7), 0], 11 + 9 * kh)
-        send(rbuf.at[kh, :, u], rbuf.at[kh, :, u], 15 + 6 * kh, place(x + 1 - 2 * u, z))
+    wait_in(rbuf.at[0, pl.ds(0, 7), 0], 11)
+    send(rbuf.at[0, :, u], rbuf.at[0, :, u], 15, place(x + 1 - 2 * u, z))
 
     wout_t = nt(eye.astype(BF16), wrecv[:, 1, pl.ds(32, 16)].reshape(128, 128)).astype(BF16)
     wait_in(hrecv.at[pl.ds(0, 7)], 16)
@@ -263,7 +269,7 @@
                 lbuf[kh, yy, core, :, pl.ds(lc * 128, 128)] = work[2 + lc, pl.ds(kh * 8 + yy, 16, stride=16), :].astype(BF16)
     send(lbuf.at[:, :, core], lbuf.at[:, :, core], 12, sibling)
     wait_in(rbuf.at[0, :, 0], 15)
-    wait_in(rbuf.at[1, :, 0], 21)
+    wait_in(rrecv.at[:, pl.ds(0, 15)], 20)
     wait_in(lbuf.at[:, :, 0], 12)
     tri = nt(rbuf[0].reshape(256, 256), lbuf[0].reshape(256, 256)) + nt(rbuf[1].reshape(256, 256), lbuf[1].reshape(256, 256))
     tsend[...] = tri.astype(BF16).reshape(8, 2, 16, 256)
@@ -344,11 +350,10 @@
     wait_out(t1.at[1, pl.ds(0, 7)], 9)
     wait_out(t2send.at[pl.ds(0, 31)], 10)
     wait_out(rrows.at[0, pl.ds(0, 7)], 11)
-    wait_out(rrows.at[1, pl.ds(0, 7)], 20)
+    wait_out(rrecv.at[:, pl.ds(0, 15)], 20)
     wait_out(lbuf.at[:, :, 0], 12)
     wait_out(msend, 13)
     wait_out(rbuf.at[0, :, 0], 15)
-    wait_out(rbuf.at[1, :, 0], 21)
     wait_out(hrecv.at[pl.ds(0, 7)], 16)
     wait_out(wrecv.at[:, 0, pl.ds(0, 32)], 17)
     wait_out(usend, 18)
@@ -375,7 +380,7 @@
     ]
     swapped = pl.pallas_call(
         kernel,
-        out_shape=jax.ShapeDtypeStruct((8, 16, RES), BF16),
+        out_shape=pltpu.VMEM((8, 16, RES), BF16),
         in_specs=[pl.BlockSpec(memory_space=pltpu.HBM)] * 9,
         out_specs=pl.BlockSpec(memory_space=pltpu.VMEM),
         scratch_shapes=[pltpu.VMEM(shape, kind) for shape, kind in scratch]

time: 57.7 us -> 55.4 us (0.960)
  the two profiles are of different devices: /device:TPU:2 before, /device:TPU:1 now
where the time goes in v6:
time: 55.4 us; the launch traced here: 55.1 us
  Pallas kernels  54.3 us (98%)
  local copies, waits for them, and re-layouts  0.73 us (1%)
    pallas_call x1, Pallas kernels, body(): pl.pallas_call(kernel, out_shape=pltpu.VMEM((8, 16, RES), BF16), in_specs...  54.3 us

profile of v6, /device:TPU:1, one launch (start us, length us, event | category | flops | bytes accessed | tf_op | source)
XLA Modules:
  0.0 55.1 jit_solution(4076488121616377324)
XLA Ops:
  0.0 54.3 %shard_map.91 = bf16[8,16,512]{2,1,0:T(8,128)(2,1)S(1)} custom-call(bf16[16,8,512]{2,1,0:T(8,128)(2,1)} %pair_in.1, s32[8,512]{1,0:T(8,128)} %mask_in.1, bf16[2,32,128]{2,1,0:T(8,128)(2,1)} %bitcast.10, f32[1,128]{1,0:T(1,128)} %bitcast.12, f32[1,128]{1,0:T(1,128)} %bitcast.13, bf16[16,128]{1,0:T(8,128)(2,1)} %bitcast.11, bf16[16,128]{1,0:T(8,128)(2,1)} %out_in.1, ...), custom_call_target="tpu_custom_call" | custom-call | tf_op jit(solution)/shard_map/pallas_call | solution.py:381
  54.3 0.7 %copy.10 = bf16[16,8,512]{2,1,0:T(8,128)(2,1)} copy(bf16[16,8,512]{2,0,1:T(8,128)(2,1)S(1)} %bitcast.9) | data formatting | bytes 262144 | tf_op jit(solution)/shard_map/transpose | solution.py:392

commit v7 on v6

--- a/solution.py
+++ b/solution.py
@@ -183,14 +183,6 @@
     def swap_y(sent, slot, sem):
         each(0, 7, lambda k: send(sent.at[to_y(k)], slot, sem, dev_y(to_y(k))))
 
-    right = operand(1).reshape(16, 8, RES)
-
-    def swap_right(kh):
-        at = kh * 256
-        rsend[kh] = jnp.concatenate([right[:, :, at:at + 128], right[:, :, at + 128:at + 256]], axis=1).astype(BF16)
-        swap_f(rsend.at[kh], rrecv.at[kh], 4 + 15 * kh)
-
-    swap_right(0)
     left = operand(0)
     for lc in range(4):
         work[lc, pl.ds(0, 128), :] = left[:, lc * 128:lc * 128 + 128]
@@ -199,6 +191,14 @@
             lsend[h, :, pl.ds(lc * 128, 128)] = work[lc, pl.ds(h, 16, stride=8), :].astype(BF16)
     swap_y(lsend, lmid.at[y], 14)
     lmid[y] = lsend[y]
+    right = operand(1).reshape(16, 8, RES)
+
+    def swap_right(kh):
+        at = kh * 256
+        rsend[kh] = jnp.concatenate([right[:, :, at:at + 128], right[:, :, at + 128:at + 256]], axis=1).astype(BF16)
+        swap_f(rsend.at[kh], rrecv.at[kh], 4 + 15 * kh)
+
+    swap_right(0)
     swap_right(1)
     hrecv[ch] = hsend[...]
 

time: 55.4 us -> 55.1 us (level)
  the two profiles are of different devices: /device:TPU:1 before, /device:TPU:8 now
where the time goes in v7:
time: 55.1 us; the launch traced here: 55 us
  Pallas kernels  54.3 us (99%)
  local copies, waits for them, and re-layouts  0.73 us (1%)
    pallas_call x1, Pallas kernels, body(): pl.pallas_call(kernel, out_shape=pltpu.VMEM((8, 16, RES), BF16), in_specs...  54.3 us

profile of v7, /device:TPU:8, one launch (start us, length us, event | category | flops | bytes accessed | tf_op | source)
XLA Modules:
  0.0 55.0 jit_solution(7193348829579024764)
XLA Ops:
  0.0 54.3 %shard_map.91 = bf16[8,16,512]{2,1,0:T(8,128)(2,1)S(1)} custom-call(bf16[16,8,512]{2,1,0:T(8,128)(2,1)} %pair_in.1, s32[8,512]{1,0:T(8,128)} %mask_in.1, bf16[2,32,128]{2,1,0:T(8,128)(2,1)} %bitcast.10, f32[1,128]{1,0:T(1,128)} %bitcast.12, f32[1,128]{1,0:T(1,128)} %bitcast.13, bf16[16,128]{1,0:T(8,128)(2,1)} %bitcast.11, bf16[16,128]{1,0:T(8,128)(2,1)} %out_in.1, ...), custom_call_target="tpu_custom_call" | custom-call | tf_op jit(solution)/shard_map/pallas_call | solution.py:381
  54.3 0.7 %copy.10 = bf16[16,8,512]{2,1,0:T(8,128)(2,1)} copy(bf16[16,8,512]{2,0,1:T(8,128)(2,1)S(1)} %bitcast.9) | data formatting | bytes 262144 | tf_op jit(solution)/shard_map/transpose | solution.py:392

commit v8 on v6

--- a/solution.py
+++ b/solution.py
@@ -191,15 +191,16 @@
         swap_f(rsend.at[kh], rrecv.at[kh], 4 + 15 * kh)
 
     swap_right(0)
+    swap_right(1)
     left = operand(0)
     for lc in range(4):
         work[lc, pl.ds(0, 128), :] = left[:, lc * 128:lc * 128 + 128]
-    for lc in range(4):
-        for h in range(8):
-            lsend[h, :, pl.ds(lc * 128, 128)] = work[lc, pl.ds(h, 16, stride=8), :].astype(BF16)
-    swap_y(lsend, lmid.at[y], 14)
-    lmid[y] = lsend[y]
-    swap_right(1)
+    for kh in range(2):
+        for lc in range(2):
+            for h in range(8):
+                lsend[kh, h, :, pl.ds(lc * 128, 128)] = work[kh * 2 + lc, pl.ds(h, 16, stride=8), :].astype(BF16)
+        swap_y(lsend.at[kh], lmid.at[kh, y], 14 + 8 * kh)
+        lmid[kh, y] = lsend[kh, y]
     hrecv[ch] = hsend[...]
 
     wait_in(wrecv.at[pl.ds(0, 7), 0, pl.ds(32, 16)], 3)
@@ -231,15 +232,18 @@
         swap_y(rrows.at[kh], rbuf.at[kh, y, u], 11 + 9 * kh)
         rbuf[kh, y, u] = rrows[kh, y]
 
+    def spread_left(kh):
+        wait_in(lmid.at[kh, pl.ds(0, 7)], 14 + 8 * kh)
+        for lc in range(2):
+            work[lc, pl.ds(256, 128), :] = lmid[kh, :, :, pl.ds(lc * 128, 128)].astype(F32).reshape(128, 128)
+        for g in range(16):
+            lrows[kh, g] = jnp.concatenate(
+                [work[lc, pl.ds(256 + g, 8, stride=16), :] for lc in range(2)], axis=0).astype(BF16)
+        swap_f(lrows.at[kh], lrecv.at[kh], 6 + 17 * kh)
+
+    spread_left(0)
     spread_right(0)
-    wait_in(lmid.at[pl.ds(0, 7)], 14)
-    for lc in range(4):
-        work[lc, pl.ds(256, 128), :] = lmid[:, :, pl.ds(lc * 128, 128)].astype(F32).reshape(128, 128)
-    for g in range(16):
-        for lc in range(2):
-            lrows[g, :, pl.ds(lc * 128, 128)] = jnp.concatenate(
-                [work[kh * 2 + lc, pl.ds(256 + g, 8, stride=16), :] for kh in range(2)], axis=0).astype(BF16)
-    swap_f(lrows, lrecv, 6)
+    spread_left(1)
     spread_right(1)
 
     wait_in(rbuf.at[0, pl.ds(0, 7), 0], 11)
@@ -260,17 +264,17 @@
                + bits(lane, 1, 1) * 4 + bits(lane, 7, 1) * 2 + bits(lane, 0, 1))
     perm = (natural == iota((256, 256), 1)).astype(BF16)
 
-    wait_in(lrecv.at[pl.ds(0, 15)], 6)
-    for lc in range(2):
-        work[2 + lc, pl.ds(0, 256), :] = lrecv[:, :, pl.ds(lc * 128, 128)].astype(F32).reshape(256, 128)
     for kh in range(2):
+        wait_in(lrecv.at[kh, pl.ds(0, 15)], 6 + 17 * kh)
+        work[2 + kh, pl.ds(0, 256), :] = lrecv[kh].astype(F32).reshape(256, 128)
         for yy in range(8):
             for lc in range(2):
-                lbuf[kh, yy, core, :, pl.ds(lc * 128, 128)] = work[2 + lc, pl.ds(kh * 8 + yy, 16, stride=16), :].astype(BF16)
-    send(lbuf.at[:, :, core], lbuf.at[:, :, core], 12, sibling)
+                lbuf[kh, yy, core, :, pl.ds(lc * 128, 128)] = work[2 + kh, pl.ds(lc * 8 + yy, 16, stride=16), :].astype(BF16)
+        send(lbuf.at[kh, :, core], lbuf.at[kh, :, core], 12 + 12 * kh, sibling)
     wait_in(rbuf.at[0, :, 0], 15)
     wait_in(rrecv.at[:, pl.ds(0, 15)], 20)
-    wait_in(lbuf.at[:, :, 0], 12)
+    wait_in(lbuf.at[0, :, 0], 12)
+    wait_in(lbuf.at[1, :, 0], 24)
     tri = nt(rbuf[0].reshape(256, 256), lbuf[0].reshape(256, 256)) + nt(rbuf[1].reshape(256, 256), lbuf[1].reshape(256, 256))
     tsend[...] = tri.astype(BF16).reshape(8, 2, 16, 256)
 
@@ -342,16 +346,19 @@
     wait_out(wrecv.at[pl.ds(0, 7), 0, pl.ds(32, 16)], 3)
     wait_out(rsend.at[0, pl.ds(0, 15)], 4)
     wait_out(rsend.at[1, pl.ds(0, 15)], 19)
-    wait_out(lsend.at[pl.ds(0, 7)], 14)
+    wait_out(lsend.at[0, pl.ds(0, 7)], 14)
+    wait_out(lsend.at[1, pl.ds(0, 7)], 22)
     wait_out(gsend.at[pl.ds(0, 15)], 5)
-    wait_out(lrows.at[pl.ds(0, 15)], 6)
+    wait_out(lrows.at[0, pl.ds(0, 15)], 6)
+    wait_out(lrows.at[1, pl.ds(0, 15)], 23)
     wait_out(g2send.at[pl.ds(0, 31)], 7)
     wait_out(t1.at[0, pl.ds(0, 7)], 8)
     wait_out(t1.at[1, pl.ds(0, 7)], 9)
     wait_out(t2send.at[pl.ds(0, 31)], 10)
     wait_out(rrows.at[0, pl.ds(0, 7)], 11)
     wait_out(rrecv.at[:, pl.ds(0, 15)], 20)
-    wait_out(lbuf.at[:, :, 0], 12)
+    wait_out(lbuf.at[0, :, 0], 12)
+    wait_out(lbuf.at[1, :, 0], 24)
     wait_out(msend, 13)
     wait_out(rbuf.at[0, :, 0], 15)
     wait_out(hrecv.at[pl.ds(0, 7)], 16)
@@ -371,7 +378,7 @@
         ((1, 128), F32), ((8, 1, 128), F32),
         ((8, 128), F32), ((8, 128), F32),
         ((2, 16, 16, 128), BF16), ((2, 16, 16, 128), BF16), ((2, 8, 16, 256), BF16), ((2, 8, 2, 16, 256), BF16),
-        ((8, 16, RES), BF16), ((8, 16, RES), BF16), ((16, 16, 256), BF16), ((16, 16, 256), BF16), ((2, 8, 2, 16, 256), BF16),
+        ((2, 8, 16, 256), BF16), ((2, 8, 16, 256), BF16), ((2, 16, 16, 128), BF16), ((2, 16, 16, 128), BF16), ((2, 8, 2, 16, 256), BF16),
         ((8, 2, 16, 256), BF16), ((2, 8, 16, 256), BF16),
         ((32, 16, 128), BF16), ((32, 16, 128), BF16),
         ((16, 32, 128), BF16), ((16, 32, 128), BF16),
@@ -384,7 +391,7 @@
         in_specs=[pl.BlockSpec(memory_space=pltpu.HBM)] * 9,
         out_specs=pl.BlockSpec(memory_space=pltpu.VMEM),
         scratch_shapes=[pltpu.VMEM(shape, kind) for shape, kind in scratch]
-        + [pltpu.SemaphoreType.DMA((9,)), pltpu.SemaphoreType.DMA((22,)), pltpu.SemaphoreType.DMA((22,))],
+        + [pltpu.SemaphoreType.DMA((9,)), pltpu.SemaphoreType.DMA((25,)), pltpu.SemaphoreType.DMA((25,))],
         compiler_params=pltpu.CompilerParams(
             collective_id=0, has_side_effects=True, vmem_limit_bytes=VMEM_LIMIT),
     )(pair, pair_mask, jnp.swapaxes(ab_weight, 1, 2).reshape(2, 32, CH), in_gain.reshape(1, CH), in_bias.reshape(1, CH),

time: 55.4 us -> 55.7 us (level)
  Pallas kernels: 54.3 us -> 54.9 us
where the time goes in v8:
time: 55.7 us; the launch traced here: 55.6 us
  Pallas kernels  54.9 us (99%)
  local copies, waits for them, and re-layouts  0.73 us (1%)
    pallas_call x1, Pallas kernels, body(): pl.pallas_call(kernel, out_shape=pltpu.VMEM((8, 16, RES), BF16), in_specs...  54.9 us

profile of v8, /device:TPU:1, one launch (start us, length us, event | category | flops | bytes accessed | tf_op | source)
XLA Modules:
  0.0 55.6 jit_solution(4933585473001010141)
XLA Ops:
  0.0 54.9 %shard_map.91 = bf16[8,16,512]{2,1,0:T(8,128)(2,1)S(1)} custom-call(bf16[16,8,512]{2,1,0:T(8,128)(2,1)} %pair_in.1, s32[8,512]{1,0:T(8,128)} %mask_in.1, bf16[2,32,128]{2,1,0:T(8,128)(2,1)} %bitcast.10, f32[1,128]{1,0:T(1,128)} %bitcast.12, f32[1,128]{1,0:T(1,128)} %bitcast.13, bf16[16,128]{1,0:T(8,128)(2,1)} %bitcast.11, bf16[16,128]{1,0:T(8,128)(2,1)} %out_in.1, ...), custom_call_target="tpu_custom_call" | custom-call | tf_op jit(solution)/shard_map/pallas_call | solution.py:388
  54.9 0.7 %copy.10 = bf16[16,8,512]{2,1,0:T(8,128)(2,1)} copy(bf16[16,8,512]{2,0,1:T(8,128)(2,1)S(1)} %bitcast.9) | data formatting | bytes 262144 | tf_op jit(solution)/shard_map/transpose | solution.py:399
